TPU v7x, 32 devices: a whole 2x2x4 slice. The times are simulated.
32 devices in a mesh: seq: 8 (over z, y), head: 4 (over x, core).
Axes of the slice: x: 2, y: 2, z: 4, core: 2. Of those that a mesh axis runs over, the one named last changes fastest.
Arguments:
- hidden_in: bfloat16 [2, 4096, 1024], P(None, 'seq'), may hold values from -6 to 6
- norm_gain: bfloat16 [1024], replicated, may hold values from 0.099609375 to 1.8984375
- query_weight: bfloat16 [1024, 512], P(None, 'head'), may hold values from -0.1875 to 0.1875
- keyvalue_matrix: bfloat16 [1024, 2, 128], replicated, may hold values from -0.1875 to 0.1875
- output_weight: bfloat16 [512, 1024], P('head'), may hold values from -2 to 2
- zgate_weight: bfloat16 [1024, 1536], P(None, 'head'), may hold values from -0.1875 to 0.1875
- inner_weight: bfloat16 [1024, 1536], P(None, 'head'), may hold values from -0.1875 to 0.1875
- state_weight: bfloat16 [1024, 256], replicated, may hold values from -0.1875 to 0.1875
- step_weight: bfloat16 [1024, 24], P(None, 'head'), may hold values from -0.5 to 0.5
- conv_inner: bfloat16 [4, 1536], P(None, 'head'), may hold values from -3 to 3
- conv_state: bfloat16 [4, 256], replicated, may hold values from -3 to 3
- step_bias: float32 [24], P('head'), may hold values from -4 to 0.5
- decay_log: float32 [24], P('head'), may hold values from -4.5 to 0.5
- skip_gain: float32 [24], P('head'), may hold values from 0.5 to 4
- ssm_gain: bfloat16 [1536], P('head'), may hold values from 0.099609375 to 1.8984375
- mixer_weight: bfloat16 [1536, 1024], P('head'), may hold values from -0.15625 to 0.15625
- mlp_gain: bfloat16 [1024], replicated, may hold values from 0.099609375 to 1.8984375
- gate_weight: bfloat16 [1024, 2048], P(None, 'head'), may hold values from -0.1875 to 0.1875
- up_weight: bfloat16 [1024, 2048], P(None, 'head'), may hold values from -0.1875 to 0.1875
- down_weight: bfloat16 [2048, 1024], P('head'), may hold values from -0.125 to 0.125
- grad_output: bfloat16 [2, 4096, 1024], P(None, 'seq'), may hold values from -6 to 6
Outputs:
- output: bfloat16 [2, 4096, 1024], P(None, 'seq')
- grad_input: float32 [2, 4096, 1024], P(None, 'seq')
- grad_norm_gain: float32 [1024], replicated
- grad_query_weight: float32 [1024, 512], P(None, 'head')
- grad_keyvalue_weight: float32 [1024, 2, 128], replicated
- grad_output_weight: float32 [512, 1024], P('head')
- grad_zgate_weight: float32 [1024, 1536], P(None, 'head')
- grad_inner_weight: float32 [1024, 1536], P(None, 'head')
- grad_state_weight: float32 [1024, 256], replicated
- grad_step_weight: float32 [1024, 24], P(None, 'head')
- grad_conv_inner: float32 [4, 1536], P(None, 'head')
- grad_conv_state: float32 [4, 256], replicated
- grad_step_bias: float32 [24], P('head')
- grad_decay_log: float32 [24], P('head')
- grad_skip_gain: float32 [24], P('head')
- grad_ssm_gain: float32 [1536], P('head')
- grad_mixer_weight: float32 [1536, 1024], P('head')
- grad_mlp_gain: float32 [1024], replicated
- grad_gate_weight: float32 [1024, 2048], P(None, 'head')
- grad_up_weight: float32 [1024, 2048], P(None, 'head')
- grad_down_weight: float32 [2048, 1024], P('head')
All inputs are finite; a program needn't handle non-finite values.
Results may differ from a plain program's by a relative error of at most 0.013.
The roundings to bfloat16 on the way count: a program that leaves them out, or rounds other values in their place, can miss the bound.
Values may be sent and summed in bfloat16 or wider, within the bound.
A program may use at most 256 MiB of HBM per device.

v0:
```python
import math

import jax
import jax.numpy as jnp
from jax import lax
from jax.sharding import PartitionSpec as P

HEADS = 8
KV_HEADS = 2
STATE = 128
SSM = 1536


HIGH_ACCURACY = lax.Precision.HIGHEST
EPSILON = 1e-05
ROPE_BASE = 100000000000.0
MASKED = -1e30


def passed_along(value, axis, steps):
    count = lax.axis_size(axis)
    first, last = (max(0, -steps), min(count, count - steps))
    return lax.ppermute(value, axis, [(source, source + steps) for source in range(first, last)])


def carried(log_totals, states, axis, backward):
    count, mine = (lax.axis_size(axis), lax.axis_index(axis))
    pieces = lax.all_gather(states.astype(jnp.bfloat16), axis)
    place = jnp.arange(count, dtype=jnp.int32)
    if backward:
        between = (place[None, :] < place[:, None]) & (place[None, :] > mine)
        used = place > mine
    else:
        between = (place[None, :] > place[:, None]) & (place[None, :] < mine)
        used = place < mine
    decay = jnp.sum(
        jnp.where(between[:, :, None, None], log_totals[None], 0.0), axis=1
    )
    weight = jnp.where(used[:, None, None], jnp.exp(decay), 0.0)
    return jnp.sum(weight[..., None, None] * pieces.astype(jnp.float32), axis=0)


def summed_share(value, axis):
    count = lax.axis_size(axis)
    pieces = value.astype(jnp.bfloat16).reshape(count, value.shape[0] // count, *value.shape[1:])
    landed = lax.all_to_all(pieces, axis, 0, 0)
    return jnp.sum(landed.astype(jnp.float32), axis=0)


def summed_rows(value, axis):
    count = lax.axis_size(axis)
    sequences, rows, width = value.shape
    pieces = value.astype(jnp.bfloat16).reshape(sequences, count, rows // count, width)
    landed = lax.all_to_all(pieces, axis, 1, 1)
    return jnp.sum(landed.astype(jnp.float32), axis=1)


def summed_everywhere(value, axis):
    share = summed_share(value, axis).astype(jnp.bfloat16)
    return lax.all_gather(share, axis, axis=0, tiled=True).astype(jnp.float32)


def matmul(left_operand, right_operand):
    return jnp.einsum(
        "std,de->ste", left_operand, right_operand, preferred_element_type=jnp.float32
    )


def matmul_back(grad, right_operand):
    return jnp.einsum("ste,de->std", grad, right_operand, preferred_element_type=jnp.float32)


def weight_grad(left_operand, grad):
    return jnp.einsum("std,ste->de", left_operand, grad, preferred_element_type=jnp.float32)


def rms_norm(values, gain):
    factor = lax.rsqrt(jnp.mean(values * values, axis=-1, keepdims=True) + EPSILON)
    return values * factor * gain


def rotate(values, positions):
    half = values.shape[-1] // 2
    freq = ROPE_BASE ** (-jnp.arange(half, dtype=jnp.float32) * 2.0 / values.shape[-1])
    angle = positions[:, None] * freq[None, :]
    cosine = jnp.cos(angle)[None, :, None, :]
    sine = jnp.sin(angle)[None, :, None, :]
    first = values[..., :half]
    second = values[..., half:]
    return jnp.concatenate(
        [first * cosine - second * sine, second * cosine + first * sine], axis=-1
    )


def block_scores(queries, keys, query_pos, key_pos, factor):
    scores = (
        jnp.einsum("sqhd,skd->shqk", queries, keys, preferred_element_type=jnp.float32) * factor
    )
    allowed = key_pos[None, :] <= query_pos[:, None]
    return jnp.where(allowed[None, None], scores, MASKED)


def conv_act(extended, conv_weight):
    rows = extended.shape[1] - (conv_weight.shape[0] - 1)
    summed = extended[:, 0:rows] * conv_weight[0]
    for tap in range(1, conv_weight.shape[0]):
        summed = summed + extended[:, tap : tap + rows] * conv_weight[tap]
    return jax.nn.silu(summed)


def ssm_inputs(extended, step_raw, conv_weight, step_bias, decay_log):
    activated = conv_act(extended, conv_weight)
    inner_width = activated.shape[-1] - 2 * STATE
    heads_here = step_raw.shape[-1]
    channels = activated[..., :inner_width].reshape(
        activated.shape[0], activated.shape[1], heads_here, inner_width // heads_here
    )
    writes = activated[..., inner_width : inner_width + STATE]
    reads = activated[..., inner_width + STATE :]
    step = jax.nn.softplus(step_raw + step_bias)
    logdecay = -step * jnp.exp(decay_log)
    return (channels, writes, reads, step, logdecay)


def intra(channels, writes, reads, step, running):
    rows = running.shape[1]
    lower = jnp.arange(rows, dtype=jnp.int32)[:, None] >= jnp.arange(rows, dtype=jnp.int32)[None, :]
    mask = lower[None, :, :, None]
    spread = running[:, :, None, :] - running[:, None, :, :]
    decay = jnp.where(mask, jnp.exp(jnp.where(mask, spread, 0.0)), 0.0)
    intersection = jnp.einsum("stn,sun->stu", reads, writes, precision=HIGH_ACCURACY)
    mixing = decay * intersection[..., None] * step[:, None, :, :]
    within = jnp.einsum("stuh,suhp->sthp", mixing, channels, precision=HIGH_ACCURACY)
    tail_weight = jnp.exp(running[:, -1:, :] - running) * step
    local = jnp.einsum("suh,suhp,sun->shpn", tail_weight, channels, writes, precision=HIGH_ACCURACY)
    return (within, local)


def inter(reads, running, state):
    return jnp.exp(running)[..., None] * jnp.einsum(
        "stn,shpn->sthp", reads, state, precision=HIGH_ACCURACY
    )


def ssm_full(extended, step_raw, conv_weight, step_bias, decay_log, skip_gain, state_in):
    channels, writes, reads, step, logdecay = ssm_inputs(
        extended, step_raw, conv_weight, step_bias, decay_log
    )
    running = running_sum(logdecay)
    within, local = intra(channels, writes, reads, step, running)
    result = within + inter(reads, running, state_in) + skip_gain[:, None] * channels
    state_end = jnp.exp(running[:, -1])[:, :, None, None] * state_in + local
    return (result, state_end)


def running_sum(values):
    rows = values.shape[1]
    lower = jnp.arange(rows, dtype=jnp.int32)[:, None] >= jnp.arange(rows, dtype=jnp.int32)[None, :]
    return jnp.einsum(
        "tu,suh->sth", lower.astype(jnp.float32), values, precision=HIGH_ACCURACY
    )


def on_device(
    hidden_in,
    norm_gain,
    query_weight,
    keyvalue_matrix,
    output_weight,
    zgate_weight,
    inner_weight,
    state_weight,
    step_weight,
    conv_inner,
    conv_state,
    step_bias,
    decay_log,
    skip_gain,
    ssm_gain,
    mixer_weight,
    mlp_gain,
    gate_weight,
    up_weight,
    down_weight,
    grad_output,
):
    sequences, rows, width = hidden_in.shape
    head_dim = keyvalue_matrix.shape[2] // 2
    heads_here = query_weight.shape[1] // head_dim
    group = HEADS // KV_HEADS
    factor = head_dim ** (-0.5)
    inner_width = inner_weight.shape[1]
    mamba_here = step_bias.shape[0]
    seq_index = lax.axis_index("seq")
    head_index = lax.axis_index("head")
    query_pos = seq_index * rows + jnp.arange(rows, dtype=jnp.int32)
    positions = query_pos.astype(jnp.float32)
    input_float = hidden_in.astype(jnp.float32)
    gain_one = norm_gain.astype(jnp.float32)
    normalized_input = rms_norm(input_float, gain_one).astype(jnp.bfloat16)
    query_raw = matmul(normalized_input, query_weight).reshape(
        sequences, rows, heads_here, head_dim
    )
    queries = rotate(query_raw, positions).astype(jnp.bfloat16)
    kv_index = head_index * heads_here // group
    own_weight = lax.dynamic_index_in_dim(keyvalue_matrix, kv_index, 1, keepdims=False)
    keyvalue_projected = matmul(normalized_input, own_weight)
    keys_own = rotate(keyvalue_projected[:, :, None, :head_dim], positions)[:, :, 0]
    keyvalue_own = jnp.concatenate([keys_own, keyvalue_projected[..., head_dim:]], axis=-1).astype(
        jnp.bfloat16
    )
    keyvalue_all = lax.all_gather(keyvalue_own, "seq", axis=1, tiled=True)
    length = keyvalue_all.shape[1]
    key_block = math.gcd(length, 512)
    blocks_needed = ((seq_index + 1) * rows + key_block - 1) // key_block

    def key_piece(index):
        start = index * key_block
        piece = lax.dynamic_slice_in_dim(keyvalue_all, start, key_block, 1)
        return (
            piece[..., :head_dim],
            piece[..., head_dim:],
            start + jnp.arange(key_block, dtype=jnp.int32),
        )

    def first_pass(index, carry):
        peak, total = carry
        keys, values, key_pos = key_piece(index)
        scores = block_scores(queries, keys, query_pos, key_pos, factor)
        new_peak = jnp.maximum(peak, jnp.max(scores, axis=-1))
        total = total * jnp.exp(peak - new_peak) + jnp.sum(
            jnp.exp(scores - new_peak[..., None]), axis=-1
        )
        return (new_peak, total)

    start_peak = jnp.full((sequences, heads_here, rows), MASKED, jnp.float32)
    peak, total = lax.fori_loop(
        0, blocks_needed, first_pass, (start_peak, jnp.zeros_like(start_peak))
    )
    log_total = peak + jnp.log(total)

    def second_pass(index, summed):
        keys, values, key_pos = key_piece(index)
        scores = block_scores(queries, keys, query_pos, key_pos, factor)
        probs = jnp.exp(scores - log_total[..., None]).astype(jnp.bfloat16)
        return summed + jnp.einsum(
            "shqk,skd->sqhd", probs, values, preferred_element_type=jnp.float32
        )

    attended_float = lax.fori_loop(
        0,
        blocks_needed,
        second_pass,
        jnp.zeros((sequences, rows, heads_here, head_dim), jnp.float32),
    )
    attended = attended_float.astype(jnp.bfloat16).reshape(sequences, rows, heads_here * head_dim)
    zgate = matmul(normalized_input, zgate_weight)
    inner = jnp.concatenate(
        [matmul(normalized_input, inner_weight), matmul(normalized_input, state_weight)], axis=-1
    )
    step_raw = matmul(normalized_input, step_weight)
    conv_weight = jnp.concatenate([conv_inner, conv_state], axis=1).astype(jnp.float32)
    taps = conv_weight.shape[0]
    before = passed_along(inner[:, rows - (taps - 1) :], "seq", 1)
    extended = jnp.concatenate([before, inner], axis=1)
    channels, writes, reads, step, logdecay = ssm_inputs(
        extended, step_raw, conv_weight, step_bias, decay_log
    )
    running = running_sum(logdecay)
    within, local = intra(channels, writes, reads, step, running)
    log_totals = lax.all_gather(running[:, -1], "seq")
    state_in = carried(log_totals, local, "seq", False)
    y_ssm = within + inter(reads, running, state_in) + skip_gain[:, None] * channels
    y_flat = y_ssm.reshape(sequences, rows, inner_width)
    gated = y_flat * jax.nn.silu(zgate)
    squares = lax.psum(jnp.sum(gated * gated, axis=-1), "head")
    ssm_factor = lax.rsqrt(squares / SSM + EPSILON)[..., None]
    gain_ssm = ssm_gain.astype(jnp.float32)
    ssm_normed = (gated * ssm_factor * gain_ssm).astype(jnp.bfloat16)
    branch_part = matmul(attended, output_weight) + matmul(ssm_normed, mixer_weight)
    quarter = rows // lax.axis_size("head")
    mixed_rows = summed_rows(branch_part, "head")
    def own_rows(value):
        return lax.dynamic_slice_in_dim(value, head_index * quarter, quarter, 1)

    input_rows = own_rows(input_float)
    hidden_rows = input_rows + mixed_rows
    gain_two = mlp_gain.astype(jnp.float32)
    normed_two_rows = rms_norm(hidden_rows, gain_two).astype(jnp.bfloat16)
    normed_two = lax.all_gather(normed_two_rows, "head", axis=1, tiled=True)
    gate = matmul(normed_two, gate_weight)
    up = matmul(normed_two, up_weight)
    activated = (jax.nn.silu(gate) * up).astype(jnp.bfloat16)
    feed_part = matmul(activated, down_weight)
    feed_own = summed_rows(feed_part, "head")
    output_own = (hidden_rows + feed_own).astype(jnp.bfloat16)
    output = lax.all_gather(output_own, "head", axis=1, tiled=True)
    act_grad = matmul_back(grad_output, down_weight)
    grad_down = weight_grad(activated, grad_output)
    gate_pull = jax.vjp(lambda gate_in, up_in: jax.nn.silu(gate_in) * up_in, gate, up)[1]
    gate_grad, up_grad = gate_pull(act_grad)
    gate_grad = gate_grad.astype(jnp.bfloat16)
    up_grad = up_grad.astype(jnp.bfloat16)
    grad_gate = weight_grad(normed_two, gate_grad)
    grad_up = weight_grad(normed_two, up_grad)
    normed_two_grad = summed_rows(
        matmul_back(gate_grad, gate_weight) + matmul_back(up_grad, up_weight), "head"
    )
    units = grad_down.shape[0]
    down_sum = summed_everywhere(grad_down, "seq")
    feed_sums = summed_everywhere(jnp.concatenate([grad_gate, grad_up], axis=1), "seq")
    norm_two_pull = jax.vjp(rms_norm, hidden_rows, gain_two)[1]
    hidden_norm_grad, grad_gain_two = norm_two_pull(normed_two_grad)
    hidden_grad = own_rows(grad_output).astype(jnp.float32) + hidden_norm_grad
    mixed_grad = lax.all_gather(
        hidden_grad.astype(jnp.bfloat16), "head", axis=1, tiled=True
    )
    grad_output_proj = weight_grad(attended, mixed_grad)
    attended_grad = (
        matmul_back(mixed_grad, output_weight)
        .astype(jnp.bfloat16)
        .reshape(sequences, rows, heads_here, head_dim)
    )
    grad_mixer = weight_grad(ssm_normed, mixed_grad)
    mixed_sums = summed_everywhere(jnp.concatenate([grad_output_proj, grad_mixer], axis=0), "seq")
    ssm_normed_grad = matmul_back(mixed_grad, mixer_weight)
    weighted = ssm_normed_grad * gain_ssm
    inner_total = lax.psum(jnp.sum(weighted * gated, axis=-1), "head")
    gated_grad = weighted * ssm_factor - gated * ssm_factor**3 * inner_total[..., None] / SSM
    grad_gain_ssm = jnp.sum(ssm_normed_grad * gated * ssm_factor, axis=(0, 1))
    gated_pull = jax.vjp(lambda y_in, z_in: y_in * jax.nn.silu(z_in), y_flat, zgate)[1]
    y_grad, zgate_grad = gated_pull(gated_grad)
    zgate_grad = zgate_grad.astype(jnp.bfloat16)
    grad_zgate = weight_grad(normalized_input, zgate_grad)
    y_grad_heads = y_grad.reshape(sequences, rows, mamba_here, inner_width // mamba_here)
    own_state_grad = jnp.einsum(
        "sth,stn,sthp->shpn", jnp.exp(running), reads, y_grad_heads, precision=HIGH_ACCURACY
    )
    state_grad = carried(log_totals, own_state_grad, "seq", True)
    ssm_pull = jax.vjp(
        ssm_full, extended, step_raw, conv_weight, step_bias, decay_log, skip_gain, state_in
    )[1]
    extended_grad, step_raw_grad, conv_grad, grad_step_bias, grad_decay_log, grad_skip, unused = (
        ssm_pull((y_grad_heads, state_grad))
    )
    before_grad = passed_along(extended_grad[:, : taps - 1], "seq", -1)
    inner_grad = extended_grad[:, taps - 1 :] + jnp.pad(
        before_grad, ((0, 0), (rows - (taps - 1), 0), (0, 0))
    )
    inner_own = inner_grad[..., :inner_width].astype(jnp.bfloat16)
    step_grad = step_raw_grad.astype(jnp.bfloat16)
    grad_inner = weight_grad(normalized_input, inner_own)
    grad_step = weight_grad(normalized_input, step_grad)
    delta = jnp.sum(attended_grad.astype(jnp.float32) * attended_float, axis=-1).transpose(0, 2, 1)

    def make_back_pass():

        def back_pass(index, carry):
            query_grad, keyvalue_grad = carry
            keys, values, key_pos = key_piece(index)
            scores = block_scores(queries, keys, query_pos, key_pos, factor)
            probs = jnp.exp(scores - log_total[..., None])
            probs_grad = jnp.einsum(
                "sqhd,skd->shqk", attended_grad, values, preferred_element_type=jnp.float32
            )
            scores_grad = (probs * (probs_grad - delta[..., None])).astype(jnp.bfloat16)
            query_grad = (
                query_grad
                + jnp.einsum(
                    "shqk,skd->sqhd", scores_grad, keys, preferred_element_type=jnp.float32
                )
                * factor
            )
            key_grad = (
                jnp.einsum(
                    "shqk,sqhd->skd", scores_grad, queries, preferred_element_type=jnp.float32
                )
                * factor
            )
            value_grad = jnp.einsum(
                "shqk,sqhd->skd",
                probs.astype(jnp.bfloat16),
                attended_grad,
                preferred_element_type=jnp.float32,
            )
            keyvalue_grad = lax.dynamic_update_slice_in_dim(
                keyvalue_grad,
                jnp.concatenate([key_grad, value_grad], axis=-1),
                index * key_block,
                1,
            )
            return (query_grad, keyvalue_grad)

        return back_pass

    query_zero = jnp.zeros((sequences, rows, heads_here, head_dim), jnp.float32)
    keyvalue_zero = jnp.zeros((sequences, length, 2 * head_dim), jnp.float32)
    query_grad, keyvalue_grad_all = lax.fori_loop(
        0, blocks_needed, make_back_pass(), (query_zero, keyvalue_zero)
    )
    keyvalue_grad_own = summed_rows(keyvalue_grad_all, "seq")
    key_raw_grad = rotate(keyvalue_grad_own[:, :, None, :head_dim], -positions)[:, :, 0]
    keyvalue_raw_grad = jnp.concatenate([key_raw_grad, keyvalue_grad_own[..., head_dim:]], axis=-1)
    chooser = (jnp.arange(KV_HEADS, dtype=jnp.int32) == kv_index).astype(jnp.float32)
    keyvalue_both = chooser[None, None, :, None] * keyvalue_raw_grad[:, :, None, :]
    query_raw_grad = (
        rotate(query_grad, -positions)
        .astype(jnp.bfloat16)
        .reshape(sequences, rows, heads_here * head_dim)
    )
    grad_query = weight_grad(normalized_input, query_raw_grad)
    normed_part = (
        matmul_back(query_raw_grad, query_weight)
        + matmul_back(zgate_grad, zgate_weight)
        + matmul_back(inner_own, inner_weight)
        + matmul_back(step_grad, step_weight)
    )
    kv_width = keyvalue_both.shape[2] * keyvalue_both.shape[3]
    together = summed_rows(
        jnp.concatenate(
            [
                normed_part,
                keyvalue_both.reshape(sequences, rows, kv_width),
                inner_grad[..., inner_width:],
            ],
            axis=-1,
        ),
        "head",
    )
    normed_sum = together[..., :width]
    low_rows = together[..., width:].astype(jnp.bfloat16)
    shared_weight = jnp.concatenate(
        [keyvalue_matrix.reshape(width, kv_width), state_weight], axis=1
    )
    grad_shared = weight_grad(own_rows(normalized_input), low_rows)
    normed_grad = normed_sum + matmul_back(low_rows, shared_weight)
    norm_one_pull = jax.vjp(rms_norm, input_rows, gain_one)[1]
    input_norm_grad, grad_gain_one = norm_one_pull(normed_grad)
    input_rows_grad = (hidden_grad + input_norm_grad).astype(jnp.bfloat16)
    grad_input = lax.all_gather(input_rows_grad, "head", axis=1, tiled=True).astype(jnp.float32)
    last_sums = summed_everywhere(
        jnp.concatenate([grad_zgate, grad_inner, grad_query], axis=1), "seq"
    )
    shared_part = summed_share(summed_share(grad_shared, "head"), "seq").astype(jnp.bfloat16)
    shared_sum = lax.all_gather(
        shared_part, ("head", "seq"), axis=0, tiled=True
    ).astype(jnp.float32)
    own_small = [
        grad_step,
        conv_grad[:, :inner_width],
        grad_step_bias,
        grad_decay_log,
        grad_skip,
        grad_gain_ssm,
    ]
    all_small = [grad_gain_one, grad_gain_two, conv_grad[:, inner_width:]]

    def unpacked(flat, likes):
        found, at = [], 0
        for like in likes:
            found.append(flat[at : at + like.size].reshape(like.shape))
            at += like.size
        return found

    own_flat = lax.psum(jnp.concatenate([part.reshape(-1) for part in own_small]), "seq")
    all_flat = lax.psum(
        jnp.concatenate([part.reshape(-1) for part in all_small]), ("seq", "head")
    )
    grad_step, conv_inner_grad, grad_step_bias, grad_decay_log, grad_skip, grad_gain_ssm = unpacked(
        own_flat, own_small
    )
    grad_gain_one, grad_gain_two, conv_state_grad = unpacked(all_flat, all_small)
    attended_width = heads_here * head_dim
    return (
        output,
        grad_input,
        grad_gain_one,
        last_sums[:, 2 * inner_width :],
        shared_sum[:, :kv_width].reshape(keyvalue_matrix.shape),
        mixed_sums[:attended_width],
        last_sums[:, :inner_width],
        last_sums[:, inner_width : 2 * inner_width],
        shared_sum[:, kv_width:],
        grad_step,
        conv_inner_grad,
        conv_state_grad,
        grad_step_bias,
        grad_decay_log,
        grad_skip,
        grad_gain_ssm,
        mixed_sums[attended_width:],
        grad_gain_two,
        feed_sums[:, :units],
        feed_sums[:, units:],
        down_sum,
    )


def solution(mesh):
    placed = (
        P(None, "seq", None),
        P(),
        P(None, "head"),
        P(),
        P("head", None),
        P(None, "head"),
        P(None, "head"),
        P(),
        P(None, "head"),
        P(None, "head"),
        P(),
        P("head"),
        P("head"),
        P("head"),
        P("head"),
        P("head", None),
        P(),
        P(None, "head"),
        P(None, "head"),
        P("head", None),
        P(None, "seq", None),
    )
    return jax.shard_map(
        on_device,
        mesh=mesh,
        in_specs=placed,
        out_specs=(
            P(None, "seq", None),
            P(None, "seq", None),
            P(),
            P(None, "head"),
            P(),
            P("head", None),
            P(None, "head"),
            P(None, "head"),
            P(),
            P(None, "head"),
            P(None, "head"),
            P(),
            P("head"),
            P("head"),
            P("head"),
            P("head"),
            P("head", None),
            P(),
            P(None, "head"),
            P(None, "head"),
            P("head", None),
        ),
        check_vma=False,
    )
```

profile of v0, /device:TPU:10, one launch (start us, length us, event | category | flops | bytes accessed | tf_op | source)
XLA Modules:
  0.0 914.4 jit_solution(2334259005817332331)
XLA Ops:
  17.3 3.4 collective-permute-start
  24.9 2.9 maximum_maximum_fusion
  28.0 3.3 fusion.66
  46.7 17.6 %all-gather = f32[16,1,6]{2,1,0:T(1,128)S(1)} all-gather(f32[2,1,6]{2,1,0:T(1,128)S(1)} %copy.251), channel_id=2, replica_groups=mesh['seq'=8,'head'=4] {'seq'}, dimensions={0}, use_global_device_ids=true | all-gather | bytes 432 | tf_op jit(solution)/shard_map/all_gather | solution.py:271
  70.8 4.4 fusion.157
  75.2 5.4 all-gather.36.cloned.1.call-done
  85.9 15.3 %fusion.77 = f32[2,512,6,64]{1,3,2,0:T(8,128)S(1)} fusion(f32[2,512,6,64]{1,3,2,0:T(8,128)S(1)} %bitcast.406, f32[2,512,6,64]{1,3,2,0:T(8,128)S(1)} %fusion.149, f32[2,512,6]{1,2,0:T(8,128)S(1)} %copy-done.114, f32[2,512,512]{2,1,0:T(8,128)S(1)} %copy-done.55, f32[2,512,6]{1,2,0:T(8,128)S(1)} %copy-done.93, pred[512,512]{1,0:T(8,128)(4,1)S(1)} %copy-done.90, ...), kind=kOutput, calls=%fused_computation.142 | convolution fusion | flops 2433220608 | bytes 7151640 | tf_op jit(solution)/shard_map/stuh,suhp->sthp/dot_general | solution.py:133
  104.1 5.9 psum.28
  110.6 20.2 %all-gather.16.cloned.1.call-done = bf16[2,4096,128]{1,2,0:T(8,128)(2,1)} async-done(((bf16[2,512,128]{1,2,0:T(8,128)(2,1)}), bf16[2,4096,128]{1,2,0:T(8,128)(2,1)}) %all-gather.16.cloned.1.call-update) | async-done | bytes 2097168 | tf_op jit(solution)/shard_map/all_gather | solution.py:212
  130.9 9.1 while.37
  140.0 8.7 while.38
  153.6 5.1 all-to-all-start
  161.7 21.2 %all-to-all-done = bf16[2,4,128,1024]{3,2,0,1:T(8,128)(2,1)} async-done(((bf16[2,4,128,1024]{3,2,0,1:T(8,128)(2,1)}), bf16[2,4,128,1024]{3,2,0,1:T(8,128)(2,1)}, u32[]{:S(2)}, u32[]{:S(2)}) %all-to-all-start) | async-done | bytes 2097184 | tf_op jit(solution)/shard_map/all_to_all | solution.py:54
  188.4 51.5 %all-gather.18.cloned.1.call-done = bf16[2,512,1024]{2,1,0:T(8,128)(2,1)} async-done(((bf16[2,128,1024]{2,1,0:T(8,128)(2,1)}), bf16[2,512,1024]{2,1,0:T(8,128)(2,1)}) %all-gather.18.cloned.1.call-update) | async-done | bytes 2097168 | tf_op jit(solution)/shard_map/all_gather | solution.py:290
  239.9 3.2 fusion.119
  244.7 3.1 multiply_convert_fusion.1
  251.3 28.0 %all_to_all.55 = bf16[2,4,128,1024]{3,2,0,1:T(8,128)(2,1)S(1)} all-to-all(bf16[2,4,128,1024]{3,2,0,1:T(8,128)(2,1)S(1)} %copy.260), channel_id=1, replica_groups=mesh['seq'=8,'head'=4] {'head'}, dimensions={1} | all-to-all | bytes 4194304 | tf_op jit(solution)/shard_map/all_to_all | solution.py:54
  282.7 3.8 bitcast_convert_fusion
  286.5 6.2 all-to-all-start.10
  292.7 12.9 %all-gather.22.cloned.1.call-done = bf16[2,512,1024]{2,1,0:T(8,128)(2,1)} async-done(((bf16[2,128,1024]{2,1,0:T(8,128)(2,1)}), bf16[2,512,1024]{2,1,0:T(8,128)(2,1)}) %all-gather.22.cloned.1.call-update) | async-done | bytes 2097168 | tf_op jit(solution)/shard_map/all_gather | solution.py:315
  305.6 4.7 multiply_reduce_fusion.7
  310.3 7.3 psum.29
  317.6 6.0 multiply_reduce_fusion.8
  323.6 3.6 fusion.107
  327.3 3.3 bitcast_convert_fusion.2
  333.5 6.1 all-to-all-start.9
  346.4 54.7 %all-to-all-done.9 = bf16[8,128,1024]{2,1,0:T(8,128)(2,1)} async-done(((bf16[8,128,1024]{2,1,0:T(8,128)(2,1)}), bf16[8,128,1024]{2,1,0:T(8,128)(2,1)}, u32[]{:S(2)}, u32[]{:S(2)}) %all-to-all-start.9) | async-done | bytes 2097184 | tf_op jit(solution)/shard_map/all_to_all | solution.py:46
  401.1 4.9 all-to-all-start.1
  413.6 20.9 %fusion.48 = (f32[2,512,6]{1,2,0:T(8,128)}, f32[2,512,6]{1,2,0:T(8,128)}, f32[2,512,6]{1,2,0:T(8,128)}, f32[2,512,512]{2,1,0:T(8,128)}) fusion(f32[2,512,6]{1,2,0:T(8,128)S(1)} %copy-done.115, f32[2,512,512]{2,1,0:T(8,128)S(1)} %copy-done.56, f32[2,512,6]{1,2,0:T(8,128)S(1)} %copy-done.94, pred[512,512]{1,0:T(8,128)(4,1)S(1)} %copy-done.91, ...), kind=kOutput, calls=%fused_computation.68 | convolution fusion | flops 2462562304 | bytes 7725056 | tf_op jit(solution)/shard_map/transpose(jvp(stuh,suhp->sthp))/dot_general | solution.py:133
  437.6 37.7 %while.39 = (s32[]{:T(128)}, f32[2,512,2,64]{1,3,2,0:T(8,128)S(1)}, bf16[2,4096,128]{2,1,0:T(8,128)(2,1)}, s32[]{:T(128)}, bf16[2,4096,128]{1,2,0:T(8,128)(2,1)}...) while((s32[]{:T(128)}, f32[2,512,2,64]{1,3,2,0:T(8,128)S(1)}, ...), condition=%wide.region_18.19_spmd.clone, body=%wide.region_17.18_spmd.clone.sunk | while | flops 682755072 | bytes 41943416 | solution.py:398
  437.7 3.7 fusion.303
  441.6 3.9 fusion.304
  450.1 3.7 fusion.303
  454.1 3.9 fusion.304
  462.6 3.7 fusion.303
  466.5 4.0 fusion.304
  475.4 4.0 copy.279
  482.3 3.3 fusion.130
  488.8 3.4 convolution_add_fusion.2
  494.4 3.6 multiply_reduce_fusion.6
  500.5 3.1 convolution_add_fusion.1
  503.6 70.3 %all-to-all-start.3 = ((bf16[2,8,512,128]{2,3,0,1:T(8,128)(2,1)}), bf16[2,8,512,128]{2,3,0,1:T(8,128)(2,1)}, u32[]{:S(2)}, u32[]{:S(2)}) async-start(bf16[2,8,512,128]{2,3,0,1:T(8,128)(2,1)} %copy.279), calls=%async_computation.3 | async-start | bytes 4194304 | tf_op jit(solution)/shard_map/all_to_all | solution.py:54
  574.0 13.8 %bitcast_add_fusion = f32[2,512,6,64]{1,3,2,0:T(8,128)S(1)} fusion(f32[2,512,6,64]{1,3,2,0:T(8,128)} %get-tuple-element.456, f32[2,512,6,64]{1,3,2,0:T(8,128)S(1)} %bitcast.414, f32[2,6,64,512]{3,2,1,0:T(8,128)S(1)} %bitcast.415, f32[2,512,6]{1,2,0:T(8,128)} %get-tuple-element.435, f32[2,512,512]{2,1,0:T(8,128)} %fusion.157, f32[2,512,6]{1,2,0:T(8,128)} %copy-done.92, ...), kind=kOutput, calls=%fused_computation.138 | convolution fusion | flops 2433220608 | bytes 8724504 | tf_op jit(solution)/shard_map/transpose(jvp(stuh,suhp->sthp))/dot_general | solution.py:133
  587.9 3.3 multiply_reduce_fusion.4
  596.5 3.5 collective-permute-start.1
  604.1 7.6 pad_add_fusion
  611.9 3.7 fusion.65
  615.6 4.4 all-to-all-done.3
  620.0 9.5 %all-to-all-start.8 = ((bf16[8,64,1024]{2,1,0:T(8,128)(2,1)}), bf16[8,64,1024]{2,1,0:T(8,128)(2,1)}, u32[]{:S(2)}, u32[]{:S(2)}) async-start(bf16[8,64,1024]{2,1,0:T(8,128)(2,1)} %bitcast.68), calls=%async_computation.8 | async-start | bytes 2097152 | tf_op jit(solution)/shard_map/all_to_all | solution.py:46
  629.4 6.5 add_convert_fusion
  643.5 3.4 pad_maximum_fusion.2
  646.9 5.1 all-to-all-done.8
  652.0 5.2 all-to-all-start.4
  661.8 30.8 %all-to-all-done.4 = bf16[2,4,128,1536]{3,2,0,1:T(8,128)(2,1)} async-done(((bf16[2,4,128,1536]{3,2,0,1:T(8,128)(2,1)}), bf16[2,4,128,1536]{3,2,0,1:T(8,128)(2,1)}, u32[]{:S(2)}, u32[]{:S(2)}) %all-to-all-start.4) | async-done | bytes 3145760 | tf_op jit(solution)/shard_map/all_to_all | solution.py:54
  700.0 3.3 fusion.101
  708.5 6.8 all-to-all-start.5
  715.9 39.9 %all-to-all-done.5 = bf16[8,128,896]{2,1,0:T(8,128)(2,1)} async-done(((bf16[8,128,896]{2,1,0:T(8,128)(2,1)}), bf16[8,128,896]{2,1,0:T(8,128)(2,1)}, u32[]{:S(2)}, u32[]{:S(2)}) %all-to-all-start.5) | async-done | bytes 1835040 | tf_op jit(solution)/shard_map/all_to_all | solution.py:46
  759.9 17.3 %all_to_all.56 = bf16[4,256,512]{2,1,0:T(8,128)(2,1)} all-to-all(bf16[4,256,512]{2,1,0:T(8,128)(2,1)S(1)} %bitcast.420), channel_id=1, replica_groups=mesh['seq'=8,'head'=4] {'head'}, dimensions={0} | all-to-all | bytes 2097152 | tf_op jit(solution)/shard_map/all_to_all | solution.py:46
  778.7 18.5 %all_to_all.57 = bf16[8,32,512]{2,1,0:T(8,128)(2,1)S(1)} all-to-all(bf16[8,32,512]{2,1,0:T(8,128)(2,1)S(1)} %bitcast.432), channel_id=1, replica_groups=mesh['seq'=8,'head'=4] {'seq'}, dimensions={0} | all-to-all | bytes 524288 | tf_op jit(solution)/shard_map/all_to_all | solution.py:46
  801.0 4.1 fusion.213
  806.5 35.4 %psum.31 = f32[8082]{0:T(1024)S(1)} all-reduce(f32[8082]{0:T(1024)S(1)} %concatenate.91), channel_id=1, replica_groups=mesh['seq'=8,'head'=4] {'seq'}, use_global_device_ids=true, to_apply=%region_50.51 | all-reduce | flops 8082 | bytes 64656 | tf_op jit(solution)/shard_map/psum | solution.py:465
  848.5 43.0 %psum.30 = f32[3072]{0:T(1024)S(1)} all-reduce(f32[3072]{0:T(1024)S(1)} %pad_maximum_fusion.9), channel_id=1, replica_groups=mesh['seq'=8,'head'=4] {'seq','head'}, use_global_device_ids=true, to_apply=%region_40.41 | all-reduce | flops 3072 | bytes 24576 | tf_op jit(solution)/shard_map/psum | solution.py:466
  892.8 4.1 convert_element_type.229
  898.6 3.2 fusion.214
  (606 shorter events, 189.0 us)
Async XLA Ops:
  7.2 237.2 %copy-start = (bf16[512,1024]{1,0:T(8,128)(2,1)S(1)}, bf16[512,1024]{1,0:T(8,128)(2,1)}, u32[]{:S(2)}) copy-start(bf16[512,1024]{1,0:T(8,128)(2,1)} %param.46) | copy-start | bytes 3145732
  7.2 73.4 %all-gather.36.cloned.1.call-start = ((), (), s32[]{:S(2)}) async-start(), calls=%async_computation.21 | async-start | bytes 1769472 | tf_op jit(solution)/shard_map/all_gather | solution.py:28
  11.4 89.7 %copy-start.5 = (bf16[2,512,1024]{2,1,0:T(8,128)(2,1)}, bf16[2,512,1024]{2,1,0:T(8,128)(2,1)S(1)}, u32[]{:S(2)}) copy-start(bf16[2,512,1024]{2,1,0:T(8,128)(2,1)S(1)} %multiply_convert_fusion) | copy-start | bytes 6291460
  14.9 5.9 copy-start.159
  14.9 5.9 copy-start.99
  14.9 5.9 copy-start.150
  16.0 7.4 copy-start.145
  16.0 7.4 copy-start.146
  17.3 6.5 collective-permute-start
  22.1 5.8 copy-start.86
  22.5 5.4 copy-start.92
  23.4 8.1 copy-start.82
  35.6 95.3 %all-gather.16.cloned.1.call-start = ((), (), s32[]{:S(2)}) async-start(), calls=%async_computation.11 | async-start | bytes 2359296 | tf_op jit(solution)/shard_map/all_gather | solution.py:212
  40.9 28.9 %copy-start.67 = (bf16[1024,128]{1,0:T(8,128)(2,1)S(1)}, bf16[1024,128]{1,0:T(8,128)(2,1)}, u32[]{:S(2)}) copy-start(bf16[1024,128]{1,0:T(8,128)(2,1)} %param.29) | copy-start | bytes 786436
  80.6 5.3 copy-start.114
  85.8 15.4 %copy-start.37 = (f32[2,512,6,64]{1,3,2,0:T(8,128)}, f32[2,512,6,64]{1,3,2,0:T(8,128)S(1)}, u32[]{:S(2)}) copy-start(f32[2,512,6,64]{1,3,2,0:T(8,128)S(1)} %fusion.149) | copy-start | bytes 4718596
  85.8 15.3 %copy-start.74 = (bf16[1024,384]{1,0:T(8,128)(2,1)S(1)}, bf16[1024,384]{1,0:T(8,128)(2,1)}, u32[]{:S(2)}) copy-start(bf16[1024,384]{1,0:T(8,128)(2,1)} %param.32) | copy-start | bytes 2359300
  140.0 8.8 copy-start.62
  153.6 5.6 copy-start.28
  153.6 29.3 %all-to-all-start = ((bf16[2,4,128,1024]{3,2,0,1:T(8,128)(2,1)}), bf16[2,4,128,1024]{3,2,0,1:T(8,128)(2,1)}, u32[]{:S(2)}, u32[]{:S(2)}) async-start(bf16[2,4,128,1024]{3,2,0,1:T(8,128)(2,1)} %copy.258), calls=%async_computation | async-start | bytes 4194304 | tf_op jit(solution)/shard_map/all_to_all | solution.py:54
  158.8 81.1 %all-gather.18.cloned.1.call-start = ((), (), s32[]{:S(2)}) async-start(), calls=%async_computation.12 | async-start | bytes 2621440 | tf_op jit(solution)/shard_map/all_gather | solution.py:290
  187.2 93.7 %copy-start.8 = (f32[2,128,1024]{2,1,0:T(8,128)}, f32[2,128,1024]{2,1,0:T(8,128)S(1)}, u32[]{:S(2)}) copy-start(f32[2,128,1024]{2,1,0:T(8,128)S(1)} %get-tuple-element.389) | copy-start | bytes 3145732
  188.3 54.8 %copy-start.64 = (bf16[1024,512]{1,0:T(8,128)(2,1)S(1)}, bf16[1024,512]{1,0:T(8,128)(2,1)}, u32[]{:S(2)}) copy-start(bf16[1024,512]{1,0:T(8,128)(2,1)} %param.44) | copy-start | bytes 3145732
  188.3 117.3 %all-gather.22.cloned.1.call-start = ((), (), s32[]{:S(2)}) async-start(), calls=%async_computation.14 | async-start | bytes 2621440 | tf_op jit(solution)/shard_map/all_gather | solution.py:315
  286.5 19.1 %copy-start.42 = (f32[2,512,384]{1,2,0:T(8,128)S(1)}, f32[2,512,384]{1,2,0:T(8,128)}, u32[]{:S(2)}) copy-start(f32[2,512,384]{1,2,0:T(8,128)} %get-tuple-element.391) | copy-start | bytes 4718596
  286.5 19.1 %copy-start.120 = (f32[384]{0:T(512)S(1)}, f32[384]{0:T(512)}, u32[]{:S(2)}) copy-start(f32[384]{0:T(512)} %convert_element_type.200) | copy-start | bytes 4612
  286.5 47.0 %all-to-all-start.10 = ((bf16[8,64,1024]{2,1,0:T(8,128)(2,1)}), bf16[8,64,1024]{2,1,0:T(8,128)(2,1)}, u32[]{:S(2)}, u32[]{:S(2)}) async-start(bf16[8,64,1024]{2,1,0:T(8,128)(2,1)} %bitcast.421), calls=%async_computation.10 | async-start | bytes 2097152 | tf_op jit(solution)/shard_map/all_to_all | solution.py:46
  292.7 24.9 %copy-start.122 = (f32[2,512]{1,0:T(2,128)S(1)}, f32[2,512]{1,0:T(2,128)}, u32[]{:S(2)}) copy-start(f32[2,512]{1,0:T(2,128)} %get-tuple-element.441) | copy-start | bytes 12292
  292.7 199.5 %all-gather.38.cloned.1.call-start = ((), (), s32[]{:S(2)}) async-start(), calls=%async_computation.22 | async-start | bytes 1769472 | tf_op jit(solution)/shard_map/all_gather | solution.py:28
  317.6 6.0 copy-start.85
  323.6 90.0 %copy-start.17 = (f32[2,512,384]{1,2,0:T(8,128)}, f32[2,512,384]{1,2,0:T(8,128)S(1)}, u32[]{:S(2)}) copy-start(f32[2,512,384]{1,2,0:T(8,128)S(1)} %get-tuple-element.384) | copy-start | bytes 4718596
  333.5 8.2 copy-start.153
  333.5 67.6 %all-to-all-start.9 = ((bf16[8,128,1024]{2,1,0:T(8,128)(2,1)}), bf16[8,128,1024]{2,1,0:T(8,128)(2,1)}, u32[]{:S(2)}, u32[]{:S(2)}) async-start(bf16[8,128,1024]{2,1,0:T(8,128)(2,1)} %pad_maximum_fusion.3), calls=%async_computation.9 | async-start | bytes 4194304 | tf_op jit(solution)/shard_map/all_to_all | solution.py:46
  339.5 458.4 %all-gather.34.cloned.1.call-start = ((), (), s32[]{:S(2)}) async-start(), calls=%async_computation.20 | async-start | bytes 1179648 | tf_op jit(solution)/shard_map/all_gather | solution.py:60
  401.1 102.5 %all-to-all-start.1 = ((bf16[2,4,128,1024]{3,2,0,1:T(8,128)(2,1)}), bf16[2,4,128,1024]{3,2,0,1:T(8,128)(2,1)}, u32[]{:S(2)}, u32[]{:S(2)}) async-start(bf16[2,4,128,1024]{3,2,0,1:T(8,128)(2,1)} %copy.259), calls=%async_computation.1 | async-start | bytes 4194304 | tf_op jit(solution)/shard_map/all_to_all | solution.py:54
  406.0 395.0 %all-gather.32.cloned.1.call-start = ((), (), s32[]{:S(2)}) async-start(), calls=%async_computation.19 | async-start | bytes 2359296 | tf_op jit(solution)/shard_map/all_gather | solution.py:60
  413.6 21.0 %copy-start.33 = (bf16[2,512,1024]{2,1,0:T(8,128)(2,1)S(1)}, bf16[2,512,1024]{2,1,0:T(8,128)(2,1)}, u32[]{:S(2)}) copy-start(bf16[2,512,1024]{2,1,0:T(8,128)(2,1)} %all-gather.22.cloned.1.call-done) | copy-start | bytes 6291460
  413.6 20.9 %copy-start.47 = (f32[2,512,2,64]{1,3,2,0:T(8,128)S(1)}, f32[2,512,2,64]{1,3,2,0:T(8,128)}, u32[]{:S(2)}) copy-start(f32[2,512,2,64]{1,3,2,0:T(8,128)} %copy-done.46) | copy-start | bytes 1572868
  413.6 20.9 %copy-start.63 = (bf16[128,1024]{1,0:T(8,128)(2,1)S(1)}, bf16[128,1024]{1,0:T(8,128)(2,1)}, u32[]{:S(2)}) copy-start(bf16[128,1024]{1,0:T(8,128)(2,1)} %param.31) | copy-start | bytes 786436
  488.8 5.3 copy-start.40
  498.0 5.6 copy-start.97
  503.6 70.3 %copy-start.18 = (f32[2,512,384]{1,2,0:T(8,128)S(1)}, f32[2,512,384]{1,2,0:T(8,128)}, u32[]{:S(2)}) copy-start(f32[2,512,384]{1,2,0:T(8,128)} %copy-done.17) | copy-start | bytes 4718596
  503.6 70.3 %copy-start.158 = (f32[6]{0:T(128)S(1)}, f32[6]{0:T(128)}, u32[]{:S(2)}) copy-start(f32[6]{0:T(128)} %param.40) | copy-start | bytes 76
  503.6 116.3 %all-to-all-start.3 = ((bf16[2,8,512,128]{2,3,0,1:T(8,128)(2,1)}), bf16[2,8,512,128]{2,3,0,1:T(8,128)(2,1)}, u32[]{:S(2)}, u32[]{:S(2)}) async-start(bf16[2,8,512,128]{2,3,0,1:T(8,128)(2,1)} %copy.279), calls=%async_computation.3 | async-start | bytes 4194304 | tf_op jit(solution)/shard_map/all_to_all | solution.py:54
  574.0 13.8 %copy-start.3 = (f32[2,515,640]{1,2,0:T(8,128)S(1)}, f32[2,515,640]{1,2,0:T(8,128)}, u32[]{:S(2)}) copy-start(f32[2,515,640]{1,2,0:T(8,128)} %copy-done.2) | copy-start | bytes 7910404
  574.0 13.8 %copy-start.12 = (f32[2,512,256]{1,2,0:T(8,128)S(1)}, f32[2,512,256]{1,2,0:T(8,128)}, u32[]{:S(2)}) copy-start(f32[2,512,256]{1,2,0:T(8,128)} %copy-done.10) | copy-start | bytes 3145732
  574.0 13.8 %copy-start.21 = (f32[2,512,384]{1,2,0:T(8,128)S(1)}, f32[2,512,384]{1,2,0:T(8,128)}, u32[]{:S(2)}) copy-start(f32[2,512,384]{1,2,0:T(8,128)} %copy-done.19) | copy-start | bytes 4718596
  574.0 13.8 %copy-start.31 = (f32[2,512,640]{1,2,0:T(8,128)S(1)}, f32[2,512,640]{1,2,0:T(8,128)}, u32[]{:S(2)}) copy-start(f32[2,512,640]{1,2,0:T(8,128)} %get-tuple-element.393) | copy-start | bytes 7864324
  574.0 13.8 %copy-start.59 = (f32[2,512,128]{1,2,0:T(8,128)S(1)}, f32[2,512,128]{1,2,0:T(8,128)}, u32[]{:S(2)}) copy-start(f32[2,512,128]{1,2,0:T(8,128)} %convolution_add_fusion.1) | copy-start | bytes 1572868
  595.9 5.4 copy-start.100
  596.5 15.1 %collective-permute-start.1 = (f32[2,3,640]{2,0,1:T(2,128)S(1)}, f32[2,3,640]{2,0,1:T(2,128)S(1)}, u32[]{:S(2)}, u32[]{:S(2)}) collective-permute-start(f32[2,3,640]{2,0,1:T(2,128)S(1)} %copy.273), channel_id=1, source_target_pairs={{4,0},{8,4},{12,8},{16,12},{20,16},{24,20},{28,24},{5,1},{9,5},{13... | collective-permute-start | bytes 46088 | tf_op jit(solution)/shard_map/ppermute | solution.py:23
  620.0 32.0 %all-to-all-start.8 = ((bf16[8,64,1024]{2,1,0:T(8,128)(2,1)}), bf16[8,64,1024]{2,1,0:T(8,128)(2,1)}, u32[]{:S(2)}, u32[]{:S(2)}) async-start(bf16[8,64,1024]{2,1,0:T(8,128)(2,1)} %bitcast.68), calls=%async_computation.8 | async-start | bytes 2097152 | tf_op jit(solution)/shard_map/all_to_all | solution.py:46
  629.4 6.5 slice-start
  646.9 12.7 %copy-start.58 = (bf16[1024,2,128]{2,1,0:T(2,128)(2,1)S(1)}, bf16[1024,2,128]{2,1,0:T(2,128)(2,1)}, u32[]{:S(2)}) copy-start(bf16[1024,2,128]{2,1,0:T(2,128)(2,1)} %param.30) | copy-start | bytes 1572868
  652.0 40.6 %all-to-all-start.4 = ((bf16[2,4,128,1536]{3,2,0,1:T(8,128)(2,1)}), bf16[2,4,128,1536]{3,2,0,1:T(8,128)(2,1)}, u32[]{:S(2)}, u32[]{:S(2)}) async-start(bf16[2,4,128,1536]{3,2,0,1:T(8,128)(2,1)} %pad_maximum_fusion.2), calls=%async_computation.4 | async-start | bytes 6291456 | tf_op jit(solution)/shard_map/all_to_all | solution.py:54
  657.2 188.0 %all-gather.30.cloned.1.call-start = ((), (), s32[]{:S(2)}) async-start(), calls=%async_computation.18 | async-start | bytes 1179648 | tf_op jit(solution)/shard_map/all_gather | solution.py:60
  659.3 233.5 %all-gather.24.cloned.1.call-start = ((), (), s32[]{:S(2)}) async-start(), calls=%async_computation.15 | async-start | bytes 2621440 | tf_op jit(solution)/shard_map/all_gather | solution.py:440
  659.7 35.6 %copy-start.112 = (f32[1024]{0:T(1024)S(1)}, f32[1024]{0:T(1024)}, u32[]{:S(2)}) copy-start(f32[1024]{0:T(1024)} %copy-done.111) | copy-start | bytes 12292
  661.8 33.5 %copy-start.81 = (bf16[1024,256]{1,0:T(8,128)(2,1)S(1)}, bf16[1024,256]{1,0:T(8,128)(2,1)}, u32[]{:S(2)}) copy-start(bf16[1024,256]{1,0:T(8,128)(2,1)} %param.34) | copy-start | bytes 1572868
  708.5 47.3 %all-to-all-start.5 = ((bf16[8,128,896]{2,1,0:T(8,128)(2,1)}), bf16[8,128,896]{2,1,0:T(8,128)(2,1)}, u32[]{:S(2)}, u32[]{:S(2)}) async-start(bf16[8,128,896]{2,1,0:T(8,128)(2,1)} %pad_maximum_fusion.4), calls=%async_computation.5 | async-start | bytes 3670016 | tf_op jit(solution)/shard_map/all_to_all | solution.py:46
  715.3 181.6 %all-gather.20.cloned.1.call-start = ((), (), s32[]{:S(2)}) async-start(), calls=%async_computation.13 | async-start | bytes 2621440 | tf_op jit(solution)/shard_map/all_gather | solution.py:297
  715.8 181.0 %all-gather.26.cloned.1.call-start = ((), (), s32[]{:S(2)}) async-start(), calls=%async_computation.16 | async-start | bytes 2064384 | tf_op jit(solution)/shard_map/all_gather | solution.py:60
  758.3 143.5 %all-gather.28.cloned.1.call-start = ((), (), s32[]{:S(2)}) async-start(), calls=%async_computation.17 | async-start | bytes 1081344 | tf_op jit(solution)/shard_map/all_gather | solution.py:445
  778.7 22.1 %copy-start.139 = (f32[384]{0:T(512)S(1)}, f32[384]{0:T(512)}, u32[]{:S(2)}) copy-start(f32[384]{0:T(512)} %get-tuple-element.383) | copy-start | bytes 4612
  (136 other events, 369.7 us)
Sparse Core Ops, SparseCore 0:
  35.7 44.8 all-gather.35
  83.2 47.6 all-gather.15
  188.5 51.3 all-gather.17
  282.8 22.7 all-gather.21
  327.4 71.6 all-gather.37
  401.1 38.7 all-gather.33
  442.0 48.9 all-gather.31
  660.7 39.9 all-gather.29
  702.8 21.4 all-gather.23
  726.2 22.5 all-gather.19
  758.4 49.8 all-gather.25
  811.9 52.0 all-gather.27
where the time goes:
time: 925 us; the launch traced here: 914 us
  waiting for transfers between devices  247 us (27%)
  matrix products  187 us (20%)
  blocking collectives  173 us (19%)
  starting transfers between devices  122 us (13%)
  other arithmetic  98.9 us (11%)
  local copies, waits for them, and re-layouts  69 us (7%)
  between operations  16.5 us (2%)
    all_to_all x4, waiting for transfers between devices, summed_share(): landed = lax.all_to_all(pieces, axis, 0, 0)  99.7 us
    all_to_all x4, starting transfers between devices, summed_rows(): landed = lax.all_to_all(pieces, axis, 1, 1)  85.5 us
    all_to_all x4, waiting for transfers between devices, summed_rows(): landed = lax.all_to_all(pieces, axis, 1, 1)  56.4 us
    all_gather x1, waiting for transfers between devices, on_device(): normed_two = lax.all_gather(normed_two_rows, 'head', axis=1, tiled=True)  51.5 us
    dot_general x3, matrix products, intra(): jnp.einsum('stuh,suhp->sthp', mixing, channels, precision=HIGH_ACCURACY)  49.9 us
    psum x1, blocking collectives, on_device(): lax.psum(jnp.concatenate([part.reshape(-1) for part in all_small]), ('seq...  43 us
    all_to_all x2, blocking collectives, summed_share(): landed = lax.all_to_all(pieces, axis, 0, 0)  35.9 us
    psum x1, blocking collectives, on_device(): lax.psum(jnp.concatenate([part.reshape(-1) for part in own_small]), 'seq')  35.4 us
  transfers between devices with their start and end apart: 22, of which 11 were waited for; matrix products, arithmetic and copies ran while one was open for 30% of the time, Pallas kernels for 0%

commit v1 on v0

v1 whole, which is shorter than its diff:
```python
import functools

import jax
import jax.numpy as jnp
from jax import lax
from jax.experimental import pallas as pl
from jax.experimental.pallas import tpu as pltpu
from jax.sharding import PartitionSpec as P

HEADS = 8
KV_HEADS = 2
STATE = 128
SSM = 1536


HIGH_ACCURACY = lax.Precision.HIGHEST
EPSILON = 1e-05
ROPE_BASE = 100000000000.0
MASKED = -1e30


def passed_along(value, axis, steps):
    count = lax.axis_size(axis)
    first, last = (max(0, -steps), min(count, count - steps))
    return lax.ppermute(value, axis, [(source, source + steps) for source in range(first, last)])


def carried(payload, axis, backward, log_totals=None):
    count, mine = (lax.axis_size(axis), lax.axis_index(axis))
    pieces = lax.all_gather(payload, axis)
    if log_totals is None:
        log_totals = jnp.sum(pieces[:, :, STATE : STATE + 3].astype(jnp.float32), axis=2)
    place = jnp.arange(count, dtype=jnp.int32)
    if backward:
        between = (place[None, :] < place[:, None]) & (place[None, :] > mine)
        used = place > mine
    else:
        between = (place[None, :] > place[:, None]) & (place[None, :] < mine)
        used = place < mine
    decay = jnp.sum(jnp.where(between[:, :, None, None], log_totals[None], 0.0), axis=1)
    weight = jnp.where(used[:, None, None], jnp.exp(decay), 0.0)
    state = jnp.sum(weight[:, :, None, :] * pieces[:, :, :STATE].astype(jnp.float32), axis=0)
    return state, log_totals


def summed_share(value, axis):
    count = lax.axis_size(axis)
    pieces = value.astype(jnp.bfloat16).reshape(count, value.shape[0] // count, *value.shape[1:])
    landed = lax.all_to_all(pieces, axis, 0, 0)
    return jnp.sum(landed.astype(jnp.float32), axis=0)


def summed_rows(value, axis):
    count = lax.axis_size(axis)
    sequences, rows, width = value.shape
    pieces = value.astype(jnp.bfloat16).reshape(sequences, count, rows // count, width)
    landed = lax.all_to_all(pieces, axis, 1, 1)
    return jnp.sum(landed.astype(jnp.float32), axis=1)


def summed_everywhere(value, axis):
    share = summed_share(value, axis).astype(jnp.bfloat16)
    return lax.all_gather(share, axis, axis=0, tiled=True).astype(jnp.float32)


def matmul(left_operand, right_operand):
    return jnp.einsum(
        "std,de->ste", left_operand, right_operand, preferred_element_type=jnp.float32
    )


def matmul_back(grad, right_operand):
    return jnp.einsum("ste,de->std", grad, right_operand, preferred_element_type=jnp.float32)


def weight_grad(left_operand, grad):
    return jnp.einsum("std,ste->de", left_operand, grad, preferred_element_type=jnp.float32)


def rms_norm(values, gain):
    factor = lax.rsqrt(jnp.mean(values * values, axis=-1, keepdims=True) + EPSILON)
    return values * factor * gain


def rotate(values, positions):
    half = values.shape[-1] // 2
    freq = ROPE_BASE ** (-jnp.arange(half, dtype=jnp.float32) * 2.0 / values.shape[-1])
    angle = positions[:, None] * freq[None, :]
    cosine = jnp.cos(angle)[None, :, None, :]
    sine = jnp.sin(angle)[None, :, None, :]
    first = values[..., :half]
    second = values[..., half:]
    return jnp.concatenate(
        [first * cosine - second * sine, second * cosine + first * sine], axis=-1
    )


CHUNK = 128
LANES = 128
HALO = 8
VMEM_BYTES = 56 * 1024 * 1024


def dot(left, right, left_dim, right_dim):
    return lax.dot_general(
        left, right, (((left_dim,), (right_dim,)), ((), ())), preferred_element_type=jnp.float32
    )


def halves(value):
    high = value.astype(jnp.bfloat16)
    return high, (value - high.astype(jnp.float32)).astype(jnp.bfloat16)


def dot3(left, right, left_dim, right_dim):
    return (
        dot(left[0], right[0], left_dim, right_dim)
        + dot(left[0], right[1], left_dim, right_dim)
        + dot(left[1], right[0], left_dim, right_dim)
    )


def exact_dot(left, right, left_dim, right_dim):
    return lax.dot_general(
        left,
        right,
        (((left_dim,), (right_dim,)), ((), ())),
        preferred_element_type=jnp.float32,
        precision=HIGH_ACCURACY,
    )


def causal(block, columns):
    key_pos = lax.broadcasted_iota(jnp.int32, (block, columns), 0)
    query_pos = lax.rem(lax.broadcasted_iota(jnp.int32, (block, columns), 1), block)
    return key_pos <= query_pos


def attention_forward_kernel(block, query_ref, kv_ref, out_ref, log_ref, acc_ref):
    blocks_before = lax.axis_index("seq")
    queries = query_ref[0]
    columns = queries.shape[0]
    acc_ref[...] = jnp.zeros_like(acc_ref)

    def step(index, carry, masked):
        peak, total = carry
        keyvalue = kv_ref[0, pl.ds(pl.multiple_of(index * block, block), block), :]
        scores = dot(keyvalue, queries, 1, 1)
        if masked:
            scores = jnp.where(causal(block, columns), scores, MASKED)
        new_peak = jnp.maximum(peak, jnp.max(scores, axis=0, keepdims=True))
        probs = jnp.exp(scores - new_peak)
        scale = jnp.exp(peak - new_peak)
        acc_ref[...] = acc_ref[...] * scale + dot(keyvalue, probs.astype(jnp.bfloat16), 0, 0)
        return new_peak, total * scale + jnp.sum(probs, axis=0, keepdims=True)

    start = (jnp.full((1, columns), MASKED, jnp.float32), jnp.zeros((1, columns), jnp.float32))
    carry = lax.fori_loop(0, blocks_before, lambda i, c: step(i, c, False), start)
    peak, total = step(blocks_before, carry, True)
    log_ref[0] = peak + jnp.log(total)
    out_ref[0] = (acc_ref[...] / total).T


def attention_forward(block, queries, keyvalue):
    sequences, columns, width = queries.shape
    length = keyvalue.shape[1]
    per_sequence = lambda s: (s, 0, 0)
    return pl.pallas_call(
        functools.partial(attention_forward_kernel, block),
        grid=(sequences,),
        in_specs=[
            pl.BlockSpec((1, columns, width), per_sequence),
            pl.BlockSpec((1, length, width), per_sequence),
        ],
        out_specs=[
            pl.BlockSpec((1, columns, width), per_sequence),
            pl.BlockSpec((1, 1, columns), per_sequence),
        ],
        out_shape=[
            jax.ShapeDtypeStruct((sequences, columns, width), jnp.float32),
            jax.ShapeDtypeStruct((sequences, 1, columns), jnp.float32),
        ],
        scratch_shapes=[pltpu.VMEM((width, columns), jnp.float32)],
        compiler_params=pltpu.CompilerParams(vmem_limit_bytes=VMEM_BYTES),
        name="attention_forward",
    )(queries, keyvalue)


def attention_backward_kernel(
    block, query_ref, grad_ref, kv_ref, log_ref, delta_ref, query_grad_ref, kv_grad_ref, acc_ref
):
    blocks_before = lax.axis_index("seq")
    queries = query_ref[0]
    grads = grad_ref[0]
    columns = queries.shape[0]
    log_total = log_ref[0]
    delta = delta_ref[0]
    acc_ref[...] = jnp.zeros_like(acc_ref)
    blocks = kv_ref.shape[1] // block

    def step(index, masked):
        place = pl.ds(pl.multiple_of(index * block, block), block)
        keyvalue = kv_ref[0, place, :]
        scores = dot(keyvalue, queries, 1, 1)
        if masked:
            scores = jnp.where(causal(block, columns), scores, MASKED)
        probs = jnp.exp(scores - log_total)
        probs_grad = dot(keyvalue, grads, 1, 1)
        scores_grad = (probs * (probs_grad - delta)).astype(jnp.bfloat16)
        acc_ref[...] += dot(keyvalue, scores_grad, 0, 0)
        kv_grad = dot(scores_grad, queries, 1, 0) + dot(probs.astype(jnp.bfloat16), grads, 1, 0)
        kv_grad_ref[0, place, :] = kv_grad.astype(kv_grad_ref.dtype)

    @pl.loop(0, blocks_before)
    def _(index):
        step(index, False)

    step(blocks_before, True)

    @pl.loop(blocks_before + 1, blocks)
    def _(index):
        place = pl.ds(pl.multiple_of(index * block, block), block)
        kv_grad_ref[0, place, :] = jnp.zeros((block, kv_grad_ref.shape[2]), kv_grad_ref.dtype)

    query_grad_ref[0] = acc_ref[...].T


def attention_backward(block, queries, grads, keyvalue, log_total, delta):
    sequences, columns, width = queries.shape
    length = keyvalue.shape[1]
    per_sequence = lambda s: (s, 0, 0)
    wide = pl.BlockSpec((1, columns, width), per_sequence)
    line = pl.BlockSpec((1, 1, columns), per_sequence)
    whole = pl.BlockSpec((1, length, width), per_sequence)
    return pl.pallas_call(
        functools.partial(attention_backward_kernel, block),
        grid=(sequences,),
        in_specs=[wide, wide, whole, line, line],
        out_specs=[wide, whole],
        out_shape=[
            jax.ShapeDtypeStruct((sequences, columns, width), jnp.float32),
            jax.ShapeDtypeStruct((sequences, length, width), jnp.bfloat16),
        ],
        scratch_shapes=[pltpu.VMEM((width, columns), jnp.float32)],
        compiler_params=pltpu.CompilerParams(vmem_limit_bytes=VMEM_BYTES),
        name="attention_backward",
    )(queries, grads, keyvalue, log_total, delta)


def spreader(width, head_width):
    lane = lax.rem(lax.broadcasted_iota(jnp.int32, (2 * LANES, width), 0), LANES)
    owner = lax.broadcasted_iota(jnp.int32, (2 * LANES, width), 1) // head_width
    return (lane == owner).astype(jnp.bfloat16)


def spread(value, ones):
    return dot(jnp.concatenate(halves(value), axis=1), ones, 1, 0)


def gathered(value, ones):
    high, low = halves(value)
    one = ones[:LANES]
    return dot(high, one, 1, 1) + dot(low, one, 1, 1)


def triangle():
    row = lax.broadcasted_iota(jnp.int32, (CHUNK, CHUNK), 0)
    column = lax.broadcasted_iota(jnp.int32, (CHUNK, CHUNK), 1)
    return row, column


def conv_window(ext_ref, conv_ref, start, rows, taps):
    total = None
    for tap in range(taps):
        term = ext_ref[pl.ds(start + HALO - taps + 1 + tap, rows), :] * conv_ref[tap : tap + 1, :]
        total = term if total is None else total + term
    return total


def load_extended(inner_ref, state_ref, halo_ref, ext_ref):
    rows, width = inner_ref.shape[1], inner_ref.shape[2]
    ext_ref[0:HALO, :] = halo_ref[0]
    ext_ref[HALO : HALO + rows, 0:width] = inner_ref[0]
    ext_ref[HALO : HALO + rows, width:] = state_ref[0]


def step_sizes(raw, params_ref):
    shifted = raw + params_ref[0:1, :]
    step = jnp.maximum(shifted, 0.0) + jnp.log1p(jnp.exp(-jnp.abs(shifted)))
    return shifted, step, -step * params_ref[1:2, :]


def running_in_chunk(logdecay):
    row, column = triangle()
    lower = (row >= column).astype(jnp.float32)
    running = exact_dot(lower, logdecay, 1, 0)
    return running, running.T


def chunk_parts(ext_ref, conv_ref, raw_ref, params_ref, ones, start, width, taps, before=None):
    pre = conv_window(ext_ref, conv_ref, start, CHUNK, taps)
    sigma = jax.nn.sigmoid(pre)
    act = pre * sigma
    raw = raw_ref[0, pl.ds(start, CHUNK), :]
    shifted, step, logdecay = step_sizes(raw, params_ref)
    running, across = running_in_chunk(logdecay)
    last = running[CHUNK - 1 : CHUNK, :]
    channels = act[:, :width]
    writes = act[:, width : width + STATE]
    reads = act[:, width + STATE :]
    narrow = [step, jnp.exp(running), jnp.exp(last - running)]
    if before is not None:
        narrow.append(jnp.exp(running + before))
    wide = spread(jnp.concatenate(narrow, axis=0), ones)
    step_wide = wide[:CHUNK]
    grown = wide[CHUNK : 2 * CHUNK]
    tail = wide[2 * CHUNK : 3 * CHUNK]
    reach = wide[3 * CHUNK :]
    return dict(
        pre=pre, sigma=sigma, shifted=shifted, step=step, logdecay=logdecay, running=running,
        across=across, last=last, channels=channels, writes=writes, reads=reads,
        step_wide=step_wide, grown=grown, tail=tail, reach=reach,
        last_factor=grown[CHUNK - 1 : CHUNK],
        stepped=channels * step_wide,
    )


def decay_block(part, head, mask):
    spread_of = part["running"][:, head : head + 1] - part["across"][head : head + 1, :]
    return jnp.exp(jnp.where(mask, spread_of, MASKED))


def ssm_forward_kernel(
    heads, taps, inner_ref, state_ref, halo_ref, raw_ref, conv_ref, params_ref, skip_ref,
    y_ref, reach_ref, reads_ref, end_ref, ext_ref
):
    rows, width = inner_ref.shape[1], inner_ref.shape[2]
    head_width = width // heads
    load_extended(inner_ref, state_ref, halo_ref, ext_ref)
    ones = spreader(width, head_width)
    row, column = triangle()
    mask = row >= column
    state = jnp.zeros((STATE, width), jnp.float32)
    before = jnp.zeros((1, LANES), jnp.float32)
    for chunk in range(rows // CHUNK):
        start = chunk * CHUNK
        part = chunk_parts(
            ext_ref, conv_ref, raw_ref, params_ref, ones, start, width, taps, before
        )
        writes, reads = halves(part["writes"]), halves(part["reads"])
        meeting = dot3(reads, writes, 1, 1)
        stepped = part["stepped"]
        pieces = []
        for head in range(heads):
            mixing = halves(decay_block(part, head, mask) * meeting)
            own = halves(stepped[:, head * head_width : (head + 1) * head_width])
            pieces.append(dot3(mixing, own, 1, 0))
        y = jnp.concatenate(pieces, axis=1) + skip_ref[0:1, :] * part["channels"]
        if chunk:
            y = y + part["grown"] * dot3(reads, halves(state), 1, 0)
        y_ref[0, pl.ds(start, CHUNK), :] = y
        reach_ref[0, pl.ds(start, CHUNK), :] = part["reach"]
        reads_ref[0, pl.ds(start, CHUNK), :] = part["reads"]
        state = part["last_factor"] * state + dot3(writes, halves(stepped * part["tail"]), 0, 0)
        before = before + part["last"]
    end_ref[0, 0:STATE, :] = state.astype(jnp.bfloat16)
    rest = spread(jnp.broadcast_to(before, (8, LANES)), ones)[0:1]
    lines = []
    for _ in range(3):
        high = rest.astype(jnp.bfloat16).astype(jnp.float32)
        lines.append(high)
        rest = rest - high
    lines.append(jnp.zeros((HALO - 3, width), jnp.float32))
    lines.append(jnp.zeros((8, width), jnp.float32))
    end_ref[0, STATE:, :] = jnp.concatenate(lines, axis=0).astype(jnp.bfloat16)


def ssm_forward(heads, taps, inner, state, halo, raw, conv, params, skip):
    sequences, rows, width = inner.shape
    total = width + 2 * STATE
    each = lambda s: (s, 0, 0)
    same = lambda s: (0, 0)
    return pl.pallas_call(
        functools.partial(ssm_forward_kernel, heads, taps),
        grid=(sequences,),
        in_specs=[
            pl.BlockSpec((1, rows, width), each),
            pl.BlockSpec((1, rows, 2 * STATE), each),
            pl.BlockSpec((1, HALO, total), each),
            pl.BlockSpec((1, rows, LANES), each),
            pl.BlockSpec((8, total), same),
            pl.BlockSpec((8, LANES), same),
            pl.BlockSpec((8, width), same),
        ],
        out_specs=[
            pl.BlockSpec((1, rows, width), each),
            pl.BlockSpec((1, rows, width), each),
            pl.BlockSpec((1, rows, STATE), each),
            pl.BlockSpec((1, STATE + 16, width), each),
        ],
        out_shape=[
            jax.ShapeDtypeStruct((sequences, rows, width), jnp.float32),
            jax.ShapeDtypeStruct((sequences, rows, width), jnp.float32),
            jax.ShapeDtypeStruct((sequences, rows, STATE), jnp.float32),
            jax.ShapeDtypeStruct((sequences, STATE + 16, width), jnp.bfloat16),
        ],
        scratch_shapes=[pltpu.VMEM((HALO + rows, total), jnp.float32)],
        compiler_params=pltpu.CompilerParams(vmem_limit_bytes=VMEM_BYTES),
        name="ssm_forward",
    )(inner, state, halo, raw, conv, params, skip)


def ssm_backward_kernel(
    heads, taps, inner_ref, state_ref, halo_ref, raw_ref, conv_ref, params_ref, skip_ref,
    y_ref, y_grad_ref, start_ref, end_grad_ref,
    ext_grad_ref, raw_grad_ref, conv_grad_ref, small_ref, ext_ref, pre_grad_ref, kept_ref
):
    rows, width = inner_ref.shape[1], inner_ref.shape[2]
    head_width = width // heads
    load_extended(inner_ref, state_ref, halo_ref, ext_ref)
    ones = spreader(width, head_width)
    row, column = triangle()
    mask = row >= column
    upper = (row <= column).astype(jnp.float32)
    chunks = rows // CHUNK
    state = start_ref[0]
    parts = []
    for chunk in range(chunks):
        start = chunk * CHUNK
        kept_ref[chunk] = state
        if chunk < chunks - 1:
            part = chunk_parts(ext_ref, conv_ref, raw_ref, params_ref, ones, start, width, taps)
            state = part["last_factor"] * state + dot3(
                halves(part["writes"]), halves(part["stepped"] * part["tail"]), 0, 0
            )
    pre_grad_ref[0:HALO, :] = jnp.zeros((HALO, pre_grad_ref.shape[1]), jnp.float32)
    pre_grad_ref[HALO + rows :, :] = jnp.zeros((HALO, pre_grad_ref.shape[1]), jnp.float32)
    grad = end_grad_ref[0]
    skip = skip_ref[0:1, :]
    decay_sum = jnp.zeros((1, LANES), jnp.float32)
    bias_sum = jnp.zeros((1, LANES), jnp.float32)
    skip_sum = jnp.zeros((1, width), jnp.float32)
    for chunk in reversed(range(chunks)):
        start = chunk * CHUNK
        part = chunk_parts(ext_ref, conv_ref, raw_ref, params_ref, ones, start, width, taps)
        channels, stepped, grown = part["channels"], part["stepped"], part["grown"]
        writes, reads = halves(part["writes"]), halves(part["reads"])
        meeting = dot3(reads, writes, 1, 1)
        y_grad = y_grad_ref[0, pl.ds(start, CHUNK), :]
        y = y_ref[0, pl.ds(start, CHUNK), :]
        state = kept_ref[chunk]
        state_halves = halves(state)
        grad_halves = halves(grad)
        meeting_grad = jnp.zeros((CHUNK, CHUNK), jnp.float32)
        pieces = []
        for head in range(heads):
            own = slice(head * head_width, (head + 1) * head_width)
            decay = decay_block(part, head, mask)
            mixing = halves(decay * meeting)
            own_grad = halves(y_grad[:, own])
            pieces.append(dot3(mixing, own_grad, 0, 0))
            meeting_grad += dot3(own_grad, halves(stepped[:, own]), 1, 1) * decay
        tail_grad = part["tail"] * dot3(writes, grad_halves, 1, 0)
        pulled = jnp.concatenate(pieces, axis=1) + tail_grad
        channels_grad = part["step_wide"] * pulled + skip * y_grad
        reached = y_grad * grown
        reached_halves = halves(reached)
        meeting_halves = halves(meeting_grad)
        ended_halves = halves(stepped * part["tail"])
        writes_grad = dot3(meeting_halves, reads, 0, 0) + dot3(ended_halves, grad_halves, 1, 1)
        reads_grad = dot3(meeting_halves, writes, 1, 0) + dot3(reached_halves, state_halves, 1, 1)
        last_factor = part["last_factor"]
        last_terms = jnp.sum(stepped * tail_grad, axis=0, keepdims=True) + last_factor * jnp.sum(
            grad * state, axis=0, keepdims=True
        )
        sums = gathered(
            jnp.concatenate(
                [
                    y_grad * (y - skip * channels) - stepped * pulled,
                    channels * pulled,
                    jnp.broadcast_to(last_terms, (8, width)),
                ],
                axis=0,
            ),
            ones,
        )
        running_grad = sums[:CHUNK]
        step_grad = sums[CHUNK : 2 * CHUNK]
        logdecay_grad = exact_dot(upper, running_grad, 1, 0) + sums[2 * CHUNK : 2 * CHUNK + 1]
        step_grad = step_grad - logdecay_grad * params_ref[1:2, :]
        raw_grad = step_grad * jax.nn.sigmoid(part["shifted"])
        raw_grad_ref[0, pl.ds(start, CHUNK), :] = raw_grad
        bias_sum += jnp.sum(raw_grad, axis=0, keepdims=True)
        decay_sum += jnp.sum(logdecay_grad * part["logdecay"], axis=0, keepdims=True)
        skip_sum += jnp.sum(y_grad * channels, axis=0, keepdims=True)
        act_grad = jnp.concatenate([channels_grad, writes_grad, reads_grad], axis=1)
        sigma = part["sigma"]
        pre_grad_ref[pl.ds(HALO + start, CHUNK), :] = (
            act_grad * sigma * (1.0 + part["pre"] * (1.0 - sigma))
        )
        grad = last_factor * grad + dot3(reads, reached_halves, 0, 0)
    small_ref[0] = jnp.concatenate(
        [
            bias_sum,
            decay_sum,
            gathered(jnp.broadcast_to(skip_sum, (8, width)), ones)[0:1],
            jnp.zeros((5, LANES), jnp.float32),
        ],
        axis=0,
    )
    count = HALO + rows
    total = None
    for tap in range(taps):
        term = pre_grad_ref[pl.ds(taps - 1 - tap, count), :] * conv_ref[tap : tap + 1, :]
        total = term if total is None else total + term
    ext_grad_ref[0] = total
    pre_grad = pre_grad_ref[pl.ds(HALO, rows), :]
    lines = [
        jnp.sum(
            pre_grad * ext_ref[pl.ds(HALO - taps + 1 + tap, rows), :], axis=0, keepdims=True
        )
        for tap in range(taps)
    ]
    lines.append(jnp.zeros((8 - taps, total.shape[1]), jnp.float32))
    conv_grad_ref[0] = jnp.concatenate(lines, axis=0)


def ssm_backward(heads, taps, inner, state, halo, raw, conv, params, skip, y, y_grad, begin, end_grad):
    sequences, rows, width = inner.shape
    total = width + 2 * STATE
    each = lambda s: (s, 0, 0)
    same = lambda s: (0, 0)
    return pl.pallas_call(
        functools.partial(ssm_backward_kernel, heads, taps),
        grid=(sequences,),
        in_specs=[
            pl.BlockSpec((1, rows, width), each),
            pl.BlockSpec((1, rows, 2 * STATE), each),
            pl.BlockSpec((1, HALO, total), each),
            pl.BlockSpec((1, rows, LANES), each),
            pl.BlockSpec((8, total), same),
            pl.BlockSpec((8, LANES), same),
            pl.BlockSpec((8, width), same),
            pl.BlockSpec((1, rows, width), each),
            pl.BlockSpec((1, rows, width), each),
            pl.BlockSpec((1, STATE, width), each),
            pl.BlockSpec((1, STATE, width), each),
        ],
        out_specs=[
            pl.BlockSpec((1, HALO + rows, total), each),
            pl.BlockSpec((1, rows, LANES), each),
            pl.BlockSpec((1, 8, total), each),
            pl.BlockSpec((1, 8, LANES), each),
        ],
        out_shape=[
            jax.ShapeDtypeStruct((sequences, HALO + rows, total), jnp.float32),
            jax.ShapeDtypeStruct((sequences, rows, LANES), jnp.float32),
            jax.ShapeDtypeStruct((sequences, 8, total), jnp.float32),
            jax.ShapeDtypeStruct((sequences, 8, LANES), jnp.float32),
        ],
        scratch_shapes=[
            pltpu.VMEM((HALO + rows, total), jnp.float32),
            pltpu.VMEM((2 * HALO + rows, total), jnp.float32),
            pltpu.VMEM((rows // CHUNK, STATE, width), jnp.float32),
        ],
        compiler_params=pltpu.CompilerParams(vmem_limit_bytes=VMEM_BYTES),
        name="ssm_backward",
    )(inner, state, halo, raw, conv, params, skip, y, y_grad, begin, end_grad)


def on_device(
    hidden_in,
    norm_gain,
    query_weight,
    keyvalue_matrix,
    output_weight,
    zgate_weight,
    inner_weight,
    state_weight,
    step_weight,
    conv_inner,
    conv_state,
    step_bias,
    decay_log,
    skip_gain,
    ssm_gain,
    mixer_weight,
    mlp_gain,
    gate_weight,
    up_weight,
    down_weight,
    grad_output,
):
    sequences, rows, width = hidden_in.shape
    head_dim = keyvalue_matrix.shape[2] // 2
    heads_here = query_weight.shape[1] // head_dim
    group = HEADS // KV_HEADS
    factor = head_dim ** (-0.5)
    inner_width = inner_weight.shape[1]
    mamba_here = step_bias.shape[0]
    seq_index = lax.axis_index("seq")
    head_index = lax.axis_index("head")
    query_pos = seq_index * rows + jnp.arange(rows, dtype=jnp.int32)
    positions = query_pos.astype(jnp.float32)
    input_float = hidden_in.astype(jnp.float32)
    gain_one = norm_gain.astype(jnp.float32)
    normalized_input = rms_norm(input_float, gain_one).astype(jnp.bfloat16)
    query_raw = matmul(normalized_input, query_weight).reshape(
        sequences, rows, heads_here, head_dim
    )
    queries = rotate(query_raw, positions).astype(jnp.bfloat16)
    kv_index = head_index * heads_here // group
    own_weight = lax.dynamic_index_in_dim(keyvalue_matrix, kv_index, 1, keepdims=False)
    keyvalue_projected = matmul(normalized_input, own_weight)
    keys_own = rotate(keyvalue_projected[:, :, None, :head_dim], positions)[:, :, 0]
    keyvalue_own = jnp.concatenate([keys_own, keyvalue_projected[..., head_dim:]], axis=-1).astype(
        jnp.bfloat16
    )
    keyvalue_all = lax.all_gather(keyvalue_own, "seq", axis=1, tiled=True)

    def by_head(value, zeros_first):
        moved = value.transpose(0, 2, 1, 3).reshape(sequences, heads_here * rows, head_dim)
        zeros = jnp.zeros_like(moved)
        return jnp.concatenate([zeros, moved] if zeros_first else [moved, zeros], axis=-1)

    def by_token(value):
        moved = value.reshape(sequences, heads_here, rows, head_dim).transpose(0, 2, 1, 3)
        return moved.reshape(sequences, rows, heads_here * head_dim)

    queries_padded = by_head(queries * jnp.asarray(factor, jnp.bfloat16), False)
    zgate = matmul(normalized_input, zgate_weight)
    inner = matmul(normalized_input, inner_weight)
    state_inner = matmul(normalized_input, state_weight)
    step_raw = matmul(normalized_input, jnp.pad(step_weight, ((0, 0), (0, LANES - mamba_here))))
    conv_weight = jnp.concatenate([conv_inner, conv_state], axis=1).astype(jnp.float32)
    taps = conv_weight.shape[0]
    conv_padded = jnp.pad(conv_weight, ((0, 8 - taps), (0, 0)))
    ends = jnp.concatenate([inner[:, rows - HALO :], state_inner[:, rows - HALO :]], axis=-1)
    halo = passed_along(ends, "seq", 1)
    lane_pad = (0, LANES - mamba_here)
    step_params = jnp.pad(
        jnp.stack([step_bias, jnp.exp(decay_log)]), ((0, 6), lane_pad)
    )
    skip_wide = jnp.broadcast_to(
        jnp.repeat(skip_gain, inner_width // mamba_here)[None], (8, inner_width)
    )
    y_local, reach, reads, state_payload = ssm_forward(
        mamba_here, taps, inner, state_inner, halo, step_raw, conv_padded, step_params, skip_wide
    )
    attended_wide, log_total = attention_forward(rows, queries_padded, keyvalue_all)
    attended = by_token(attended_wide[..., head_dim:].astype(jnp.bfloat16))
    state_in, log_totals = carried(state_payload, "seq", False)
    y_flat = y_local + reach * jnp.einsum(
        "stn,snw->stw", reads, state_in, precision=HIGH_ACCURACY
    )
    gated = y_flat * jax.nn.silu(zgate)
    squares = lax.psum(jnp.sum(gated * gated, axis=-1), "head")
    ssm_factor = lax.rsqrt(squares / SSM + EPSILON)[..., None]
    gain_ssm = ssm_gain.astype(jnp.float32)
    ssm_normed = (gated * ssm_factor * gain_ssm).astype(jnp.bfloat16)
    branch_part = matmul(attended, output_weight) + matmul(ssm_normed, mixer_weight)
    quarter = rows // lax.axis_size("head")
    mixed_rows = summed_rows(branch_part, "head")
    def own_rows(value):
        return lax.dynamic_slice_in_dim(value, head_index * quarter, quarter, 1)

    input_rows = own_rows(input_float)
    hidden_rows = input_rows + mixed_rows
    gain_two = mlp_gain.astype(jnp.float32)
    normed_two_rows = rms_norm(hidden_rows, gain_two).astype(jnp.bfloat16)
    normed_two = lax.all_gather(normed_two_rows, "head", axis=1, tiled=True)
    gate = matmul(normed_two, gate_weight)
    up = matmul(normed_two, up_weight)
    activated = (jax.nn.silu(gate) * up).astype(jnp.bfloat16)
    feed_part = matmul(activated, down_weight)
    feed_own = summed_rows(feed_part, "head")
    output_own = (hidden_rows + feed_own).astype(jnp.bfloat16)
    output = lax.all_gather(output_own, "head", axis=1, tiled=True)
    act_grad = matmul_back(grad_output, down_weight)
    grad_down = weight_grad(activated, grad_output)
    gate_pull = jax.vjp(lambda gate_in, up_in: jax.nn.silu(gate_in) * up_in, gate, up)[1]
    gate_grad, up_grad = gate_pull(act_grad)
    gate_grad = gate_grad.astype(jnp.bfloat16)
    up_grad = up_grad.astype(jnp.bfloat16)
    grad_gate = weight_grad(normed_two, gate_grad)
    grad_up = weight_grad(normed_two, up_grad)
    normed_two_grad = summed_rows(
        matmul_back(gate_grad, gate_weight) + matmul_back(up_grad, up_weight), "head"
    )
    units = grad_down.shape[0]
    down_sum = summed_everywhere(grad_down, "seq")
    feed_sums = summed_everywhere(jnp.concatenate([grad_gate, grad_up], axis=1), "seq")
    norm_two_pull = jax.vjp(rms_norm, hidden_rows, gain_two)[1]
    hidden_norm_grad, grad_gain_two = norm_two_pull(normed_two_grad)
    hidden_grad = own_rows(grad_output).astype(jnp.float32) + hidden_norm_grad
    mixed_grad = lax.all_gather(
        hidden_grad.astype(jnp.bfloat16), "head", axis=1, tiled=True
    )
    grad_output_proj = weight_grad(attended, mixed_grad)
    attended_grad = matmul_back(mixed_grad, output_weight).astype(jnp.bfloat16)
    grads_padded = by_head(attended_grad.reshape(sequences, rows, heads_here, head_dim), True)
    delta = jnp.sum(grads_padded.astype(jnp.float32) * attended_wide, axis=-1)[:, None, :]
    grad_mixer = weight_grad(ssm_normed, mixed_grad)
    mixed_sums = summed_everywhere(jnp.concatenate([grad_output_proj, grad_mixer], axis=0), "seq")
    ssm_normed_grad = matmul_back(mixed_grad, mixer_weight)
    weighted = ssm_normed_grad * gain_ssm
    inner_total = lax.psum(jnp.sum(weighted * gated, axis=-1), "head")
    gated_grad = weighted * ssm_factor - gated * ssm_factor**3 * inner_total[..., None] / SSM
    grad_gain_ssm = jnp.sum(ssm_normed_grad * gated * ssm_factor, axis=(0, 1))
    gated_pull = jax.vjp(lambda y_in, z_in: y_in * jax.nn.silu(z_in), y_flat, zgate)[1]
    y_grad, zgate_grad = gated_pull(gated_grad)
    zgate_grad = zgate_grad.astype(jnp.bfloat16)
    grad_zgate = weight_grad(normalized_input, zgate_grad)
    own_state_grad = jnp.einsum(
        "stn,stw->snw", reads, reach * y_grad, precision=HIGH_ACCURACY
    )
    state_grad, _ = carried(own_state_grad.astype(jnp.bfloat16), "seq", True, log_totals)
    extended_grad, raw_grad, conv_grad, small_grad = ssm_backward(
        mamba_here, taps, inner, state_inner, halo, step_raw, conv_padded, step_params,
        skip_wide, y_flat, y_grad, state_in, state_grad,
    )
    step_raw_grad = raw_grad[..., :mamba_here]
    conv_grad = jnp.sum(conv_grad, axis=0)[:taps]
    small_grad = jnp.sum(small_grad, axis=0)[:, :mamba_here]
    grad_step_bias, grad_decay_log, grad_skip = small_grad[0], small_grad[1], small_grad[2]
    before_grad = passed_along(extended_grad[:, :HALO], "seq", -1)
    inner_grad = extended_grad[:, HALO:] + jnp.pad(before_grad, ((0, 0), (rows - HALO, 0), (0, 0)))
    inner_own = inner_grad[..., :inner_width].astype(jnp.bfloat16)
    step_grad = step_raw_grad.astype(jnp.bfloat16)
    grad_inner = weight_grad(normalized_input, inner_own)
    grad_step = weight_grad(normalized_input, step_grad)
    query_grad, keyvalue_grad_all = attention_backward(
        rows, queries_padded, grads_padded, keyvalue_all, log_total, delta
    )
    query_grad = by_token(query_grad[..., :head_dim]).reshape(
        sequences, rows, heads_here, head_dim
    ) * factor
    keyvalue_grad_own = summed_rows(keyvalue_grad_all, "seq")
    key_raw_grad = rotate(keyvalue_grad_own[:, :, None, :head_dim], -positions)[:, :, 0]
    keyvalue_raw_grad = jnp.concatenate([key_raw_grad, keyvalue_grad_own[..., head_dim:]], axis=-1)
    chooser = (jnp.arange(KV_HEADS, dtype=jnp.int32) == kv_index).astype(jnp.float32)
    keyvalue_both = chooser[None, None, :, None] * keyvalue_raw_grad[:, :, None, :]
    query_raw_grad = (
        rotate(query_grad, -positions)
        .astype(jnp.bfloat16)
        .reshape(sequences, rows, heads_here * head_dim)
    )
    grad_query = weight_grad(normalized_input, query_raw_grad)
    normed_part = (
        matmul_back(query_raw_grad, query_weight)
        + matmul_back(zgate_grad, zgate_weight)
        + matmul_back(inner_own, inner_weight)
        + matmul_back(step_grad, step_weight)
    )
    kv_width = keyvalue_both.shape[2] * keyvalue_both.shape[3]
    together = summed_rows(
        jnp.concatenate(
            [
                normed_part,
                keyvalue_both.reshape(sequences, rows, kv_width),
                inner_grad[..., inner_width:],
            ],
            axis=-1,
        ),
        "head",
    )
    normed_sum = together[..., :width]
    low_rows = together[..., width:].astype(jnp.bfloat16)
    shared_weight = jnp.concatenate(
        [keyvalue_matrix.reshape(width, kv_width), state_weight], axis=1
    )
    grad_shared = weight_grad(own_rows(normalized_input), low_rows)
    normed_grad = normed_sum + matmul_back(low_rows, shared_weight)
    norm_one_pull = jax.vjp(rms_norm, input_rows, gain_one)[1]
    input_norm_grad, grad_gain_one = norm_one_pull(normed_grad)
    input_rows_grad = (hidden_grad + input_norm_grad).astype(jnp.bfloat16)
    grad_input = lax.all_gather(input_rows_grad, "head", axis=1, tiled=True).astype(jnp.float32)
    own_small = [
        grad_step,
        conv_grad[:, :inner_width],
        grad_step_bias,
        grad_decay_log,
        grad_skip,
        grad_gain_ssm,
    ]
    all_small = [grad_gain_one, grad_gain_two, conv_grad[:, inner_width:]]
    all_flat = lax.psum(jnp.concatenate([part.reshape(-1) for part in all_small]), "head")
    flat = jnp.concatenate([part.reshape(-1) for part in own_small] + [all_flat])
    extra = -(-flat.shape[0] // width // LANES) * LANES
    flat = jnp.pad(flat, (0, extra * width - flat.shape[0])).reshape(width, extra)
    last_sums = summed_everywhere(
        jnp.concatenate([grad_zgate, grad_inner, grad_query, flat], axis=1), "seq"
    )
    small_sums = last_sums[:, last_sums.shape[1] - extra :].reshape(-1)
    shared_part = summed_share(summed_share(grad_shared, "head"), "seq").astype(jnp.bfloat16)
    shared_sum = lax.all_gather(
        shared_part, ("head", "seq"), axis=0, tiled=True
    ).astype(jnp.float32)
    def unpacked(flat, likes):
        found, at = [], 0
        for like in likes:
            found.append(flat[at : at + like.size].reshape(like.shape))
            at += like.size
        return found

    (
        grad_step,
        conv_inner_grad,
        grad_step_bias,
        grad_decay_log,
        grad_skip,
        grad_gain_ssm,
        grad_gain_one,
        grad_gain_two,
        conv_state_grad,
    ) = unpacked(small_sums, own_small + all_small)
    attended_width = heads_here * head_dim
    return (
        output,
        grad_input,
        grad_gain_one,
        last_sums[:, 2 * inner_width : last_sums.shape[1] - extra],
        shared_sum[:, :kv_width].reshape(keyvalue_matrix.shape),
        mixed_sums[:attended_width],
        last_sums[:, :inner_width],
        last_sums[:, inner_width : 2 * inner_width],
        shared_sum[:, kv_width:],
        grad_step,
        conv_inner_grad,
        conv_state_grad,
        grad_step_bias,
        grad_decay_log,
        grad_skip,
        grad_gain_ssm,
        mixed_sums[attended_width:],
        grad_gain_two,
        feed_sums[:, :units],
        feed_sums[:, units:],
        down_sum,
    )


def solution(mesh):
    placed = (
        P(None, "seq", None),
        P(),
        P(None, "head"),
        P(),
        P("head", None),
        P(None, "head"),
        P(None, "head"),
        P(),
        P(None, "head"),
        P(None, "head"),
        P(),
        P("head"),
        P("head"),
        P("head"),
        P("head"),
        P("head", None),
        P(),
        P(None, "head"),
        P(None, "head"),
        P("head", None),
        P(None, "seq", None),
    )
    return jax.shard_map(
        on_device,
        mesh=mesh,
        in_specs=placed,
        out_specs=(
            P(None, "seq", None),
            P(None, "seq", None),
            P(),
            P(None, "head"),
            P(),
            P("head", None),
            P(None, "head"),
            P(None, "head"),
            P(),
            P(None, "head"),
            P(None, "head"),
            P(),
            P("head"),
            P("head"),
            P("head"),
            P("head"),
            P("head", None),
            P(),
            P(None, "head"),
            P(None, "head"),
            P("head", None),
        ),
        check_vma=False,
    )
```

time: 925 us -> 781 us (0.84)
  blocking collectives: 173 us -> 52.1 us
  matrix products: 187 us -> 82.8 us
  waiting for transfers between devices: 247 us -> 340 us
  Pallas kernels: 0 us -> 64.4 us
  starting transfers between devices: 122 us -> 67.4 us
  other arithmetic: 98.9 us -> 80.2 us
    dot_general x35 -> x2, matrix products: 124 us -> 3.43 us  [the longest x1 2.05 us: on_device(): jnp.einsum('stn,stw->snw', reads, reach * y_grad, precision=HIGH_ACCURACY)]
    psum x2 -> x1, blocking collectives: 78.5 us -> 11.4 us  [on_device(): lax.psum(jnp.concatenate([part.reshape(-1) for part in all_small]), 'head')]
    pallas_call x0 -> x4, Pallas kernels: none -> 64.4 us  [the longest x1 28.3 us: ssm_backward(): pl.pallas_call(functools.partial(ssm_backward_kernel, heads, taps), grid=...]
    all_to_all x4, starting transfers between devices: 85.5 us -> 24 us  [summed_rows(): landed = lax.all_to_all(pieces, axis, 1, 1)]
    all_gather x4, waiting for transfers between devices: 0.05 us -> 47.8 us  [summed_everywhere(): return lax.all_gather(share, axis, axis=0, tiled=True).astype(jnp.float32)]
    all_to_all x2 -> x0, blocking collectives: 35.9 us -> none  [summed_share(): landed = lax.all_to_all(pieces, axis, 0, 0)]
    all_gather x1, waiting for transfers between devices: 51.5 us -> 30.5 us  [on_device(): normed_two = lax.all_gather(normed_two_rows, 'head', axis=1, tiled=True)]
    all_to_all x4, waiting for transfers between devices: 56.4 us -> 76.6 us  [summed_rows(): landed = lax.all_to_all(pieces, axis, 1, 1)]
  transfers between devices with their start and end apart: 22 -> 24, of which waited for: 11 -> 14; matrix products, arithmetic and copies ran while one was open for 30% -> 23% of each run, Pallas kernels for 0% -> 6%
where the time goes in v1:
time: 781 us; the launch traced here: 771 us
  waiting for transfers between devices  340 us (44%)
  matrix products  82.8 us (11%)
  other arithmetic  80.2 us (10%)
  local copies, waits for them, and re-layouts  68.2 us (9%)
  starting transfers between devices  67.4 us (9%)
  Pallas kernels  64.4 us (8%)
  blocking collectives  52.1 us (7%)
  between operations  15.7 us (2%)
    all_to_all x6, waiting for transfers between devices, summed_share(): landed = lax.all_to_all(pieces, axis, 0, 0)  113 us
    all_to_all x4, waiting for transfers between devices, summed_rows(): landed = lax.all_to_all(pieces, axis, 1, 1)  76.6 us
    all_gather x4, waiting for transfers between devices, summed_everywhere(): return lax.all_gather(share, axis, axis=0, tiled=True).astype(jnp.float32)  47.8 us
    all_gather x1, waiting for transfers between devices, on_device(): keyvalue_all = lax.all_gather(keyvalue_own, 'seq', axis=1, tiled=True)  35.3 us
    all_to_all x6, starting transfers between devices, summed_share(): landed = lax.all_to_all(pieces, axis, 0, 0)  35.1 us
    dot_general x10, matrix products, matmul_back(): jnp.einsum('ste,de->std', grad, right_operand, preferred_element_type=jnp...  31.4 us
    all_gather x1, waiting for transfers between devices, on_device(): normed_two = lax.all_gather(normed_two_rows, 'head', axis=1, tiled=True)  30.5 us
    dot_general x10, matrix products, weight_grad(): jnp.einsum('std,ste->de', left_operand, grad, preferred_element_type=jnp....  28.5 us
  transfers between devices with their start and end apart: 24, of which 14 were waited for; matrix products, arithmetic and copies ran while one was open for 23% of the time, Pallas kernels for 6%

profile of v1, /device:TPU:10, one launch (start us, length us, event | category | flops | bytes accessed | tf_op | source)
XLA Modules:
  0.0 771.0 jit_solution(8102257967230132147)
XLA Ops:
  14.5 3.6 collective-permute-start
  22.0 10.9 %ssm_forward.1 = (f32[2,512,384]{2,1,0:T(8,128)}, f32[2,512,384]{2,1,0:T(8,128)}, f32[2,512,128]{2,1,0:T(8,128)}, bf16[2,144,384]{2,1,0:T(8,128)(2,1)}) custom-call(f32[2,512,384]{2,1,0:T(8,128)} %copy-done.15, f32[2,512,256]{2,1,0:T(8,128)} %copy-done.13, f32[2,8,640]{2,1,0:T(8,128)} %copy-done.55, f32[2,512,128]{2,1,0:T(8,128)} %fusion.58.raw_ref, ...), custom_call_target="tpu_custom_call" | custom-call | tf_op jit(solution)/shard_map/ssm_forward/pallas_call | solution.py:383
  55.9 23.9 %all-gather.35.cloned.1.call-done = bf16[16,144,384]{2,1,0:T(8,128)(2,1)} async-done(((bf16[2,144,384]{2,1,0:T(8,128)(2,1)}), bf16[16,144,384]{2,1,0:T(8,128)(2,1)}) %all-gather.35.cloned.1.call-update) | async-done | bytes 1769488 | tf_op jit(solution)/shard_map/all_gather | solution.py:30
  85.1 3.7 multiply_reduce_fusion.4
  88.8 6.2 psum.21
  95.0 35.3 %all-gather.15.cloned.1.call-done.kv_ref = bf16[2,4096,128]{2,1,0:T(8,128)(2,1)} async-done(((bf16[2,512,128]{2,1,0:T(8,128)(2,1)}), bf16[2,4096,128]{2,1,0:T(8,128)(2,1)}) %all-gather.15.cloned.1.call-update) | async-done | bytes 2097168 | tf_op jit(solution)/shard_map/all_gather | solution.py:619
  130.3 8.0 %attention_forward.1 = (f32[2,1024,128]{2,1,0:T(8,128)}, f32[2,1,1024]{2,1,0:T(1,128)}) custom-call(bf16[2,1024,128]{2,1,0:T(8,128)(2,1)} %concatenate.77.query_ref, bf16[2,4096,128]{2,1,0:T(8,128)(2,1)} %all-gather.15.cloned.1.call-done.kv_ref), custom_call_target="tpu_custom_call" | custom-call | tf_op jit(solution)/shard_map/attention_forward/pallas_call | solution.py:168
  146.6 5.0 all-to-all-start
  151.6 4.1 convert_element_type.180
  155.6 20.0 %all-to-all-done = bf16[2,4,128,1024]{3,2,0,1:T(8,128)(2,1)} async-done(((bf16[2,4,128,1024]{3,2,0,1:T(8,128)(2,1)}), bf16[2,4,128,1024]{3,2,0,1:T(8,128)(2,1)}, u32[]{:S(2)}, u32[]{:S(2)}) %all-to-all-start) | async-done | bytes 2097184 | tf_op jit(solution)/shard_map/all_to_all | solution.py:57
  181.9 30.5 %all-gather.17.cloned.1.call-done = bf16[2,512,1024]{2,1,0:T(8,128)(2,1)} async-done(((bf16[2,128,1024]{2,1,0:T(8,128)(2,1)}), bf16[2,512,1024]{2,1,0:T(8,128)(2,1)}) %all-gather.17.cloned.1.call-update) | async-done | bytes 2097168 | tf_op jit(solution)/shard_map/all_gather | solution.py:671
  212.4 3.2 fusion.34
  217.3 3.1 multiply_convert_fusion.1
  223.9 28.2 %all_to_all.55 = bf16[2,4,128,1024]{3,2,0,1:T(8,128)(2,1)S(1)} all-to-all(bf16[2,4,128,1024]{3,2,0,1:T(8,128)(2,1)S(1)} %copy.291), channel_id=1, replica_groups=mesh['seq'=8,'head'=4] {'head'}, dimensions={1} | all-to-all | bytes 4194304 | tf_op jit(solution)/shard_map/all_to_all | solution.py:57
  255.4 2.5 convolution_convert_fusion
  259.4 6.1 all-to-all-start.1
  265.5 4.3 bitcast_convert_fusion
  272.2 27.3 %all-to-all-done.1 = bf16[2,4,128,1024]{3,2,0,1:T(8,128)(2,1)} async-done(((bf16[2,4,128,1024]{3,2,0,1:T(8,128)(2,1)}), bf16[2,4,128,1024]{3,2,0,1:T(8,128)(2,1)}, u32[]{:S(2)}, u32[]{:S(2)}) %all-to-all-start.1) | async-done | bytes 2097184 | tf_op jit(solution)/shard_map/all_to_all | solution.py:57
  299.4 6.1 all-to-all-start.10
  305.5 5.3 multiply_reduce_fusion.2
  310.8 6.3 psum.22
  317.1 4.3 fusion.10
  324.6 3.2 bitcast_convert_fusion.1
  329.5 6.2 all-to-all-start.9
  337.0 2.4 convolution_convert_fusion.1
  343.1 17.3 %attention_backward.1 = (f32[2,1024,128]{2,1,0:T(8,128)}, bf16[2,4096,128]{2,1,0:T(8,128)(2,1)}) custom-call(bf16[2,1024,128]{2,1,0:T(8,128)(2,1)} %concatenate.77.query_ref, bf16[2,1024,128]{2,1,0:T(8,128)(2,1)} %concatenate.82.grad_ref, bf16[2,4096,128]{2,1,0:T(8,128)(2,1)} %all-gather.15.cloned.1.call-done.kv_ref, ...), custom_call_target="tpu_custom_call" | custom-call | tf_op jit(solution)/shard_map/attention_backward/pallas_call | solution.py:235
  360.3 3.1 copy.298
  363.5 35.0 %all-to-all-done.9 = bf16[8,128,1024]{2,1,0:T(8,128)(2,1)} async-done(((bf16[8,128,1024]{2,1,0:T(8,128)(2,1)}), bf16[8,128,1024]{2,1,0:T(8,128)(2,1)}, u32[]{:S(2)}, u32[]{:S(2)}) %all-to-all-start.9) | async-done | bytes 2097184 | tf_op jit(solution)/shard_map/all_to_all | solution.py:49
  398.4 7.7 %all-to-all-start.3 = ((bf16[2,8,512,128]{3,2,0,1:T(8,128)(2,1)}), bf16[2,8,512,128]{3,2,0,1:T(8,128)(2,1)}, u32[]{:S(2)}, u32[]{:S(2)}) async-start(bf16[2,8,512,128]{3,2,0,1:T(8,128)(2,1)} %copy.298), calls=%async_computation.3 | async-start | bytes 4194304 | tf_op jit(solution)/shard_map/all_to_all | solution.py:57
  409.2 2.7 reduce_sum.326
  415.6 2.8 fusion.17
  420.5 2.7 fusion.65
  423.2 3.3 fusion.43
  426.6 2.5 fusion.end_grad_ref
  429.1 28.3 %ssm_backward.1 = (f32[2,520,640]{2,1,0:T(8,128)}, f32[2,512,128]{2,1,0:T(8,128)}, f32[2,8,640]{2,1,0:T(8,128)}, f32[2,8,128]{2,1,0:T(8,128)}) custom-call(f32[2,512,384]{2,1,0:T(8,128)} %copy-done.15, f32[2,512,256]{2,1,0:T(8,128)} %copy-done.13, f32[2,8,640]{2,1,0:T(8,128)} %copy-done.55, f32[2,512,128]{2,1,0:T(8,128)} %fusion.58.raw_ref, ...), custom_call_target="tpu_custom_call" | custom-call | tf_op jit(solution)/shard_map/ssm_backward/pallas_call | solution.py:533
  458.1 3.6 collective-permute-start.1
  462.7 2.4 collective-permute-done.1
  468.1 3.4 fusion.47
  471.5 5.3 all-to-all-start.8
  476.8 6.7 add_convert_fusion
  487.8 3.1 mul.578
  495.8 18.9 %all-to-all-done.8 = bf16[8,64,1024]{2,1,0:T(8,128)(2,1)} async-done(((bf16[8,64,1024]{2,1,0:T(8,128)(2,1)}), bf16[8,64,1024]{2,1,0:T(8,128)(2,1)}, u32[]{:S(2)}, u32[]{:S(2)}) %all-to-all-start.8) | async-done | bytes 1048608 | tf_op jit(solution)/shard_map/all_to_all | solution.py:49
  514.6 5.2 all-to-all-start.4
  522.9 3.1 convert_reduce_fusion.3
  526.0 29.3 %all-to-all-done.4 = bf16[2,4,128,1536]{3,2,0,1:T(8,128)(2,1)} async-done(((bf16[2,4,128,1536]{3,2,0,1:T(8,128)(2,1)}), bf16[2,4,128,1536]{3,2,0,1:T(8,128)(2,1)}, u32[]{:S(2)}, u32[]{:S(2)}) %all-to-all-start.4) | async-done | bytes 3145760 | tf_op jit(solution)/shard_map/all_to_all | solution.py:57
  555.2 2.7 convert_reduce_fusion
  560.6 2.6 fusion.27
  563.1 3.3 bitcast_convert_fusion.6
  566.4 2.5 bitcast_convert_fusion.3
  569.0 5.2 all-to-all-start.6
  574.7 3.2 fusion.18
  582.9 15.2 %all-to-all-done.6 = bf16[4,256,512]{2,1,0:T(8,128)(2,1)S(1)} async-done(((bf16[4,256,512]{2,1,0:T(8,128)(2,1)}), bf16[4,256,512]{2,1,0:T(8,128)(2,1)S(1)}, u32[]{:S(2)}, u32[]{:S(2)}) %all-to-all-start.6) | async-done | bytes 1048608 | tf_op jit(solution)/shard_map/all_to_all | solution.py:49
  599.0 6.3 all-to-all-start.7
  605.3 3.3 bitcast_convert_fusion.5
  608.6 11.4 %psum.23 = bf16[3072]{0:T(1024)(128)(2,1)S(1)} all-reduce(f32[3072]{0:T(1024)S(1)} %pad_maximum_fusion.7), channel_id=1, replica_groups=mesh['seq'=8,'head'=4] {'head'}, use_global_device_ids=true, to_apply=%region_25.26 | all-reduce | flops 3072 | bytes 18432 | tf_op jit(solution)/shard_map/psum | solution.py:787
  620.1 3.0 pad_maximum_fusion.1
  623.8 6.0 all-to-all-start.5
  631.5 44.0 %all-to-all-done.5 = bf16[8,128,1024]{2,1,0:T(8,128)(2,1)S(1)} async-done(((bf16[8,128,1024]{2,1,0:T(8,128)(2,1)}), bf16[8,128,1024]{2,1,0:T(8,128)(2,1)S(1)}, u32[]{:S(2)}, u32[]{:S(2)}) %all-to-all-start.5) | async-done | bytes 2097184 | tf_op jit(solution)/shard_map/all_to_all | solution.py:49
  676.7 2.8 convert_element_type.221
  679.5 4.1 fusion.85
  683.6 2.5 slice.256
  687.0 4.1 convert_element_type.213
  691.1 9.6 %all-gather.27.cloned.1.call-done = bf16[1024,512]{1,0:T(8,128)(2,1)} async-done(((bf16[32,512]{1,0:T(8,128)(2,1)}), bf16[1024,512]{1,0:T(8,128)(2,1)}) %all-gather.27.cloned.1.call-update) | async-done | bytes 1048592 | tf_op jit(solution)/shard_map/all_gather | solution.py:796
  704.5 47.8 %all-gather.25.cloned.1.call-done = bf16[1024,1024]{1,0:T(8,128)(2,1)} async-done(((bf16[128,1024]{1,0:T(8,128)(2,1)}), bf16[1024,1024]{1,0:T(8,128)(2,1)}) %all-gather.25.cloned.1.call-update) | async-done | bytes 2097168 | tf_op jit(solution)/shard_map/all_gather | solution.py:63
  (341 shorter events, 129.5 us)
Async XLA Ops:
  7.2 209.8 %copy-start = (bf16[512,1024]{1,0:T(8,128)(2,1)S(1)}, bf16[512,1024]{1,0:T(8,128)(2,1)}, u32[]{:S(2)}) copy-start(bf16[512,1024]{1,0:T(8,128)(2,1)} %param.40) | copy-start | bytes 3145732
  7.2 72.6 %all-gather.35.cloned.1.call-start = ((), (), s32[]{:S(2)}) async-start(), calls=%async_computation.21 | async-start | bytes 1990656 | tf_op jit(solution)/shard_map/all_gather | solution.py:30
  12.7 5.4 copy-start.58
  14.4 5.4 copy-start.82
  14.4 5.4 copy-start.70
  14.4 5.4 copy-start.73
  14.4 6.0 copy-start.78
  14.5 6.6 copy-start.79
  14.5 6.9 collective-permute-start
  33.0 97.4 %all-gather.15.cloned.1.call-start = ((), (), s32[]{:S(2)}) async-start(), calls=%async_computation.11 | async-start | bytes 2359296 | tf_op jit(solution)/shard_map/all_gather | solution.py:619
  45.0 5.4 copy-start.75
  79.9 3.8 copy-start.31
  81.7 3.4 copy-start.16
  81.7 3.4 copy-start.17
  83.7 5.1 copy-start.23
  146.6 29.1 %all-to-all-start = ((bf16[2,4,128,1024]{3,2,0,1:T(8,128)(2,1)}), bf16[2,4,128,1024]{3,2,0,1:T(8,128)(2,1)}, u32[]{:S(2)}, u32[]{:S(2)}) async-start(bf16[2,4,128,1024]{3,2,0,1:T(8,128)(2,1)} %copy.289), calls=%async_computation | async-start | bytes 4194304 | tf_op jit(solution)/shard_map/all_to_all | solution.py:57
  151.5 60.9 %all-gather.17.cloned.1.call-start = ((), (), s32[]{:S(2)}) async-start(), calls=%async_computation.12 | async-start | bytes 2621440 | tf_op jit(solution)/shard_map/all_gather | solution.py:671
  151.6 4.1 copy-start.74
  179.9 74.3 %copy-start.61 = (f32[2,128]{1,0:T(2,128)}, f32[2,128]{1,0:T(2,128)S(1)}, u32[]{:S(2)}) copy-start(f32[2,128]{1,0:T(2,128)S(1)} %fusion.78) | copy-start | bytes 3076
  181.9 123.6 %all-gather.21.cloned.1.call-start = ((), (), s32[]{:S(2)}) async-start(), calls=%async_computation.14 | async-start | bytes 2621440 | tf_op jit(solution)/shard_map/all_gather | solution.py:696
  254.3 3.6 copy-start.66
  259.4 40.0 %all-to-all-start.1 = ((bf16[2,4,128,1024]{3,2,0,1:T(8,128)(2,1)}), bf16[2,4,128,1024]{3,2,0,1:T(8,128)(2,1)}, u32[]{:S(2)}, u32[]{:S(2)}) async-start(bf16[2,4,128,1024]{3,2,0,1:T(8,128)(2,1)} %copy.290), calls=%async_computation.1 | async-start | bytes 4194304 | tf_op jit(solution)/shard_map/all_to_all | solution.py:57
  265.5 4.3 copy-start.41
  265.5 4.3 copy-start.81
  299.4 30.0 %all-to-all-start.10 = ((bf16[8,64,1024]{2,1,0:T(8,128)(2,1)}), bf16[8,64,1024]{2,1,0:T(8,128)(2,1)S(1)}, u32[]{:S(2)}, u32[]{:S(2)}) async-start(bf16[8,64,1024]{2,1,0:T(8,128)(2,1)} %bitcast.207), calls=%async_computation.10 | async-start | bytes 2097152 | tf_op jit(solution)/shard_map/all_to_all | solution.py:49
  305.5 121.1 %all-gather.37.cloned.1.call-start = ((), (), s32[]{:S(2)}) async-start(), calls=%async_computation.22 | async-start | bytes 1769472 | tf_op jit(solution)/shard_map/all_gather | solution.py:30
  317.1 5.4 copy-start.18
  317.1 5.4 copy-start.32
  329.5 69.0 %all-to-all-start.9 = ((bf16[8,128,1024]{2,1,0:T(8,128)(2,1)}), bf16[8,128,1024]{2,1,0:T(8,128)(2,1)}, u32[]{:S(2)}, u32[]{:S(2)}) async-start(bf16[8,128,1024]{2,1,0:T(8,128)(2,1)} %pad_maximum_fusion.2), calls=%async_computation.9 | async-start | bytes 4194304 | tf_op jit(solution)/shard_map/all_to_all | solution.py:49
  335.7 341.0 %all-gather.33.cloned.1.call-start = ((), (), s32[]{:S(2)}) async-start(), calls=%async_computation.20 | async-start | bytes 1179648 | tf_op jit(solution)/shard_map/all_gather | solution.py:63
  363.4 42.7 %copy-start.51 = (f32[512,32]{0,1:T(8,128)S(1)}, f32[512,32]{0,1:T(8,128)}, u32[]{:S(2)}) copy-start(f32[512,32]{0,1:T(8,128)} %get-tuple-element.218) | copy-start | bytes 196612
  363.4 43.5 %copy-start.52 = (f32[512,32]{0,1:T(8,128)S(1)}, f32[512,32]{0,1:T(8,128)}, u32[]{:S(2)}) copy-start(f32[512,32]{0,1:T(8,128)} %get-tuple-element.219) | copy-start | bytes 196612
  363.4 45.0 %copy-start.57 = (f32[8,2,384]{2,1,0:T(2,128)S(1)}, f32[8,2,384]{2,1,0:T(2,128)}, u32[]{:S(2)}) copy-start(f32[8,2,384]{2,1,0:T(2,128)} %get-tuple-element.177) | copy-start | bytes 73732
  363.4 45.0 %copy-start.72 = (pred[8]{0:T(512)(128)(4,1)S(1)}, pred[8]{0:T(512)(128)(4,1)}, u32[]{:S(2)}) copy-start(pred[8]{0:T(512)(128)(4,1)} %copy-done.71) | copy-start | bytes 28
  398.4 73.1 %all-to-all-start.3 = ((bf16[2,8,512,128]{3,2,0,1:T(8,128)(2,1)}), bf16[2,8,512,128]{3,2,0,1:T(8,128)(2,1)}, u32[]{:S(2)}, u32[]{:S(2)}) async-start(bf16[2,8,512,128]{3,2,0,1:T(8,128)(2,1)} %copy.298), calls=%async_computation.3 | async-start | bytes 4194304 | tf_op jit(solution)/shard_map/all_to_all | solution.py:57
  406.1 273.3 %all-gather.31.cloned.1.call-start = ((), (), s32[]{:S(2)}) async-start(), calls=%async_computation.19 | async-start | bytes 2359296 | tf_op jit(solution)/shard_map/all_gather | solution.py:63
  414.3 4.1 copy-start.6
  414.3 4.1 copy-start.8
  415.6 4.9 copy-start.35
  429.1 32.6 %copy-start.25 = (bf16[384,1024]{1,0:T(8,128)(2,1)S(1)}, bf16[384,1024]{1,0:T(8,128)(2,1)}, u32[]{:S(2)}) copy-start(bf16[384,1024]{1,0:T(8,128)(2,1)} %bitcast_convert_fusion.4) | copy-start | bytes 2359300
  429.1 32.6 %copy-start.43 = (bf16[128,1024]{1,0:T(8,128)(2,1)S(1)}, bf16[128,1024]{1,0:T(8,128)(2,1)}, u32[]{:S(2)}) copy-start(bf16[128,1024]{1,0:T(8,128)(2,1)} %fusion.17) | copy-start | bytes 786436
  458.1 7.0 collective-permute-start.1
  462.7 5.4 copy-start.50
  471.5 5.3 copy-start.28
  471.5 5.3 copy-start.59
  471.5 43.2 %all-to-all-start.8 = ((bf16[8,64,1024]{2,1,0:T(8,128)(2,1)}), bf16[8,64,1024]{2,1,0:T(8,128)(2,1)}, u32[]{:S(2)}, u32[]{:S(2)}) async-start(bf16[8,64,1024]{2,1,0:T(8,128)(2,1)} %bitcast.63), calls=%async_computation.8 | async-start | bytes 2097152 | tf_op jit(solution)/shard_map/all_to_all | solution.py:49
  486.4 4.4 copy-start.77
  487.8 4.4 slice-start
  495.8 26.3 %copy-start.30 = (bf16[1024,2,128]{2,1,0:T(2,128)(2,1)S(1)}, bf16[1024,2,128]{2,1,0:T(2,128)(2,1)}, u32[]{:S(2)}) copy-start(bf16[1024,2,128]{2,1,0:T(2,128)(2,1)} %param.24) | copy-start | bytes 1572868
  514.6 40.6 %all-to-all-start.4 = ((bf16[2,4,128,1536]{3,2,0,1:T(8,128)(2,1)}), bf16[2,4,128,1536]{3,2,0,1:T(8,128)(2,1)}, u32[]{:S(2)}, u32[]{:S(2)}) async-start(bf16[2,4,128,1536]{3,2,0,1:T(8,128)(2,1)} %copy.337), calls=%async_computation.4 | async-start | bytes 6291456 | tf_op jit(solution)/shard_map/all_to_all | solution.py:57
  519.9 163.8 %all-gather.29.cloned.1.call-start = ((), (), s32[]{:S(2)}) async-start(), calls=%async_computation.18 | async-start | bytes 1179648 | tf_op jit(solution)/shard_map/all_gather | solution.py:63
  522.0 165.0 %all-gather.23.cloned.1.call-start = ((), (), s32[]{:S(2)}) async-start(), calls=%async_computation.15 | async-start | bytes 2621440 | tf_op jit(solution)/shard_map/all_gather | solution.py:777
  566.4 8.3 %copy-start.36 = (bf16[2,512,2,64]{1,3,2,0:T(8,128)(2,1)S(1)}, bf16[2,512,2,64]{1,3,2,0:T(8,128)(2,1)}, u32[]{:S(2)}) copy-start(bf16[2,512,2,64]{1,3,2,0:T(8,128)(2,1)} %copy-done.35) | copy-start | bytes 786436
  566.4 8.3 %copy-start.65 = (f32[2,512]{1,0:T(2,128)S(1)}, f32[2,512]{1,0:T(2,128)}, u32[]{:S(2)}) copy-start(f32[2,512]{1,0:T(2,128)} %copy-done.64) | copy-start | bytes 12292
  569.0 29.1 %all-to-all-start.6 = ((bf16[4,256,512]{2,1,0:T(8,128)(2,1)}), bf16[4,256,512]{2,1,0:T(8,128)(2,1)S(1)}, u32[]{:S(2)}, u32[]{:S(2)}) async-start(bf16[4,256,512]{2,1,0:T(8,128)(2,1)} %bitcast.58), calls=%async_computation.6 | async-start | bytes 2097152 | tf_op jit(solution)/shard_map/all_to_all | solution.py:49
  574.1 116.9 %all-gather.19.cloned.1.call-start = ((), (), s32[]{:S(2)}) async-start(), calls=%async_computation.13 | async-start | bytes 2621440 | tf_op jit(solution)/shard_map/all_gather | solution.py:678
  574.7 4.4 copy-start.60
  577.9 4.9 copy-start.69
  599.0 24.2 %all-to-all-start.7 = ((bf16[8,32,512]{2,1,0:T(8,128)(2,1)}), bf16[8,32,512]{2,1,0:T(8,128)(2,1)S(1)}, u32[]{:S(2)}, u32[]{:S(2)}) async-start(bf16[8,32,512]{2,1,0:T(8,128)(2,1)} %bitcast.223), calls=%async_computation.7 | async-start | bytes 524288 | tf_op jit(solution)/shard_map/all_to_all | solution.py:49
  605.3 14.7 %copy-start.76 = (bf16[384]{0:T(512)(128)(2,1)S(1)}, bf16[384]{0:T(512)(128)(2,1)}, u32[]{:S(2)}) copy-start(bf16[384]{0:T(512)(128)(2,1)} %get-tuple-element.173) | copy-start | bytes 2308
  623.8 51.7 %all-to-all-start.5 = ((bf16[8,128,1024]{2,1,0:T(8,128)(2,1)}), bf16[8,128,1024]{2,1,0:T(8,128)(2,1)S(1)}, u32[]{:S(2)}, u32[]{:S(2)}) async-start(bf16[8,128,1024]{2,1,0:T(8,128)(2,1)} %pad_maximum_fusion.1), calls=%async_computation.5 | async-start | bytes 4194304 | tf_op jit(solution)/shard_map/all_to_all | solution.py:49
  629.8 70.9 %all-gather.27.cloned.1.call-start = ((), (), s32[]{:S(2)}) async-start(), calls=%async_computation.17 | async-start | bytes 1081344 | tf_op jit(solution)/shard_map/all_gather | solution.py:796
  631.5 120.9 %all-gather.25.cloned.1.call-start = ((), (), s32[]{:S(2)}) async-start(), calls=%async_computation.16 | async-start | bytes 2359296 | tf_op jit(solution)/shard_map/all_gather | solution.py:63
  752.3 4.8 copy-start.11
  (44 other events, 88.4 us)
Sparse Core Ops, SparseCore 0:
  33.1 46.7 all-gather.34
  82.6 47.6 all-gather.14
  182.0 30.3 all-gather.16
  255.5 32.8 all-gather.20
  324.7 71.5 all-gather.36
  398.4 61.6 all-gather.32
  462.2 60.6 all-gather.30
  525.0 39.6 all-gather.28
  566.9 32.6 all-gather.22
  601.6 21.9 all-gather.18
  634.3 66.3 all-gather.26
  703.3 49.0 all-gather.24
